TPU v7x, 512 devices: a whole 4x4x16 slice. The times are simulated.
512 devices in a mesh: gx: 4 (over x), gy: 8 (over z_lo, core), gz: 16 (over z_hi, y).
Axes of the slice: x: 4, y: 4, z: 16 (z_hi: 4, z_lo: 4; z = z_hi * 4 + z_lo), core: 2. Of those that a mesh axis runs over, the one named last changes fastest.
Arguments:
- offsets: float32 [3, 8, 16, 32, 16], P(None, 'gx', 'gy', 'gz'), may hold values from 0 to 6
- species: int32 [8, 16, 32, 16], P('gx', 'gy', 'gz'), may hold values from 0 to 88
- counts: int32 [8, 16, 32], P('gx', 'gy', 'gz'), may hold values from 2 to 16, as said below
- edges: int32 [2, 4, 8, 16, 1024], P(None, 'gx', 'gy', 'gz'), may hold values from -1 to 1023, as said below
- emb: bfloat16 [89, 128], replicated, may hold values from -6 to 6
- rad_in: bfloat16 [2, 8, 64], replicated, may hold values from -2 to 2
- rad_hid: bfloat16 [2, 64, 64], replicated, may hold values from -0.75 to 0.75
- rad_out: bfloat16 [2, 64, 256], replicated, may hold values from -0.75 to 0.75
- mix_one: bfloat16 [2, 128, 128], replicated, may hold values from -0.5 to 0.5
- project: bfloat16 [2, 128, 128], replicated, may hold values from -0.5 to 0.5
- mix_two: bfloat16 [128, 128], replicated, may hold values from -0.5 to 0.5
- readout: float32 [128], replicated, may hold values from -0.5 to 0.5
Outputs:
- forces: float32 [3, 8, 16, 32, 16], P(None, 'gx', 'gy', 'gz')
- energy: float32 [], replicated
Inputs may be any that keep to these rules, and one draw needn't show every extreme that they name: `counts`: every cell holds 2 to 16 atoms, in its lowest slots; some cell holds exactly 16. `edges`: each occupied slot of a device's cells is the target of exactly 8 entries, in random order; other entries are -1 in both rows. A source is an occupied slot of the target's cell or of one of its 26 neighbouring cells, never the target itself, and may repeat.
All inputs are finite; a program needn't handle non-finite values.
Results may differ from a plain program's by a relative error of at most 0.015.
Values may be sent and summed in bfloat16 or wider, within the bound.
A program may use at most 128 MiB of HBM per device.

v0:
```python
import jax
import jax.numpy as jnp
from jax import lax
from jax.sharding import PartitionSpec as P

DEG = 8


cell_length = 6.0


def with_halo(shard, sides, width):
    for axis, dim in sides:
        size, length = (lax.axis_size(axis), shard.shape[dim])
        up = [(i, (i + 1) % size) for i in range(size)]
        down = [(j, i) for i, j in up]
        last = lax.slice_in_dim(shard, length - width, length, axis=dim)
        initial = lax.slice_in_dim(shard, 0, width, axis=dim)
        before = lax.ppermute(last, axis, up)
        after = lax.ppermute(initial, axis, down)
        shard = jnp.concatenate([before, shard, after], axis=dim)
    return shard


def radial(relative, w_in, w_hid, w_out):
    squared = jnp.sum(relative * relative, axis=1, keepdims=True)
    basis_count = w_in.shape[0]
    inverse_widths = 0.1 * 30.0 ** (jnp.arange(basis_count, dtype=jnp.float32) / (basis_count - 1))
    basis_values = jnp.exp(-squared * inverse_widths[None, :]).astype(jnp.bfloat16)
    hidden = jax.nn.silu(jnp.dot(basis_values, w_in, preferred_element_type=jnp.float32)).astype(
        jnp.bfloat16
    )
    hidden = jax.nn.silu(jnp.dot(hidden, w_hid, preferred_element_type=jnp.float32)).astype(
        jnp.bfloat16
    )
    return jnp.dot(hidden, w_out, preferred_element_type=jnp.float32)


def messages_one(relative, source_rows, radial_out, channels):
    scalar_part = radial_out[:, :channels] * source_rows
    vector_part = radial_out[:, channels:] * source_rows
    return jnp.concatenate(
        [
            scalar_part,
            vector_part * relative[:, 0:1],
            vector_part * relative[:, 1:2],
            vector_part * relative[:, 2:3],
        ],
        axis=1,
    )


def messages_two(relative, source_rows, radial_out, channels):
    inner_sum = (
        relative[:, 0:1] * source_rows[:, channels : 2 * channels]
        + relative[:, 1:2] * source_rows[:, 2 * channels : 3 * channels]
        + relative[:, 2:3] * source_rows[:, 3 * channels :]
    )
    return (
        radial_out[:, :channels] * source_rows[:, :channels] + radial_out[:, channels:] * inner_sum
    )


def embedding(species_ids, emb):
    onehot = (species_ids[:, None] == jnp.arange(emb.shape[0], dtype=jnp.int32)[None, :]).astype(
        jnp.bfloat16
    )
    return jnp.dot(onehot, emb, preferred_element_type=jnp.float32)


def node_one(summed, mix_one, channels):
    scaled = (summed / DEG**0.5).astype(jnp.bfloat16)
    scalars = jax.nn.silu(
        jnp.dot(scaled[:, :channels], mix_one[0], preferred_element_type=jnp.float32)
    )
    vectors = jnp.dot(
        scaled[:, channels:].reshape(-1, channels), mix_one[1], preferred_element_type=jnp.float32
    ).reshape(scaled.shape[0], 3 * channels)
    return (scalars, vectors)


def project_up(features, project, channels):
    scalars = jnp.dot(features[:, :channels], project[0], preferred_element_type=jnp.float32)
    vectors = jnp.dot(
        features[:, channels:].reshape(-1, channels), project[1], preferred_element_type=jnp.float32
    ).reshape(features.shape[0], 3 * channels)
    return jnp.concatenate([scalars, vectors], axis=1).astype(jnp.bfloat16)


def project_back(grads, project, channels):
    scalars = jnp.dot(
        grads[:, :channels], project[0].astype(jnp.float32).T, precision=lax.Precision.HIGHEST
    )
    vectors = jnp.dot(
        grads[:, channels:].reshape(-1, channels),
        project[1].astype(jnp.float32).T,
        precision=lax.Precision.HIGHEST,
    ).reshape(grads.shape[0], 3 * channels)
    return jnp.concatenate([scalars, vectors], axis=1)


def node_two(summed, scalars, mix_two, readout, occupied):
    scaled = (summed / DEG**0.5).astype(jnp.bfloat16)
    mixed_rows = jnp.dot(scaled, mix_two, preferred_element_type=jnp.float32) + scalars
    per_atom = jnp.dot(jax.nn.silu(mixed_rows), readout, precision=lax.Precision.HIGHEST)
    return jnp.sum(per_atom * occupied)


def fold_back(extended, first_axis):
    for offset in range(3):
        axis_index = first_axis + offset
        inner_size = extended.shape[axis_index] - 4
        middle = lax.slice_in_dim(extended, 2, inner_size + 2, axis=axis_index)
        lower_rim = lax.slice_in_dim(extended, 0, 1, axis=axis_index)
        upper_rim = lax.slice_in_dim(extended, inner_size + 3, inner_size + 4, axis=axis_index)
        low_widths = [(0, 0)] * extended.ndim
        high_widths = [(0, 0)] * extended.ndim
        low_widths[axis_index] = (0, inner_size - 1)
        high_widths[axis_index] = (inner_size - 1, 0)
        extended = middle + jnp.pad(lower_rim, low_widths) + jnp.pad(upper_rim, high_widths)
    return extended


def body(
    offsets,
    species,
    counts,
    edges,
    emb,
    rad_in,
    rad_hid,
    rad_out,
    mix_one,
    project,
    mix_two,
    readout,
):
    _, cells_x, cells_y, cells_z, slot_count = offsets.shape
    channels = emb.shape[1]
    own_count = cells_x * cells_y * cells_z * slot_count
    geometry = jnp.concatenate([offsets, species.astype(jnp.float32)[None]], axis=0)
    padded = with_halo(geometry, (("gx", 1), ("gy", 2), ("gz", 3)), 1)
    near_positions = padded[:3].reshape(3, -1).T
    near_species = padded[3].reshape(-1).astype(jnp.int32)
    own_positions = offsets.reshape(3, -1).T
    occupied = (
        (jnp.arange(slot_count, dtype=jnp.int32)[None, None, None, :] < counts[..., None])
        .reshape(-1)
        .astype(jnp.float32)
    )
    near_table = embedding(near_species, emb)
    flat_edges = edges.reshape(2, -1)
    raw_target = flat_edges[0]
    valid_edge = (raw_target >= 0).astype(jnp.float32)
    target = jnp.maximum(raw_target, 0)
    source = jnp.maximum(flat_edges[1], 0)
    cell_target = target // slot_count
    target_z = cell_target % cells_z
    target_y = cell_target // cells_z % cells_y
    target_x = cell_target // (cells_z * cells_y)
    cell_source = source // slot_count
    padded_z = cell_source % (cells_z + 2)
    padded_y = cell_source // (cells_z + 2) % (cells_y + 2)
    padded_x = cell_source // ((cells_z + 2) * (cells_y + 2))
    cell_shift = jnp.stack(
        [padded_x - 1 - target_x, padded_y - 1 - target_y, padded_z - 1 - target_z], axis=1
    ).astype(jnp.float32)
    block_rows = DEG * cells_y * cells_z * slot_count
    block_count = target.shape[0] // block_rows
    pieces = (
        target.reshape(block_count, block_rows),
        source.reshape(block_count, block_rows),
        cell_shift.reshape(block_count, block_rows, 3),
        valid_edge.reshape(block_count, block_rows),
    )

    def gather_terms(which_layer, own_moved, near_moved, features):

        def one_block(running, block_data):
            local_target, local_source, shift_rows, valid_rows = block_data
            relative = (
                shift_rows + (near_moved[local_source] - own_moved[local_target]) / cell_length
            )
            radial_out = radial(
                relative, rad_in[which_layer], rad_hid[which_layer], rad_out[which_layer]
            )
            if which_layer == 0:
                message = messages_one(relative, features[local_source], radial_out, channels)
            else:
                message = messages_two(relative, features[local_source], radial_out, channels)
            message = message * valid_rows[:, None]
            return (running + jax.ops.segment_sum(message, local_target, own_count), None)

        width_out = 4 * channels if which_layer == 0 else channels
        initial = jnp.zeros((own_count, width_out), jnp.float32)
        summed, _ = lax.scan(one_block, initial, pieces)
        return summed

    summed_one, back_one = jax.vjp(
        lambda own_moved, near_moved: gather_terms(0, own_moved, near_moved, near_table),
        own_positions,
        near_positions,
    )
    (scalars, vectors), back_node_one = jax.vjp(
        lambda summed: node_one(summed, mix_one, channels), summed_one
    )
    hidden_state = jnp.concatenate([scalars, vectors], axis=1).astype(jnp.bfloat16)
    arriving = with_halo(
        hidden_state.reshape(cells_x, cells_y, cells_z, slot_count, 4 * channels),
        (("gx", 0), ("gy", 1), ("gz", 2)),
        1,
    ).reshape(-1, 4 * channels)
    lifted = project_up(arriving, project, channels).astype(jnp.float32)
    summed_two, back_two = jax.vjp(
        lambda own_moved, near_moved, lifted_in: gather_terms(1, own_moved, near_moved, lifted_in),
        own_positions,
        near_positions,
        lifted,
    )
    local_energy, back_node_two = jax.vjp(
        lambda summed, kept_scalars: node_two(summed, kept_scalars, mix_two, readout, occupied),
        summed_two,
        scalars,
    )
    total_energy = lax.psum(local_energy, ("gx", "gy", "gz"))
    site_total = own_count * lax.axis_size("gx") * lax.axis_size("gy") * lax.axis_size("gz")
    energy = total_energy / site_total
    grad_summed, grad_scalars = back_node_two(jnp.ones((), jnp.float32))
    grad_own_two, grad_near_two, grad_lifted = back_two(grad_summed)
    returning = project_back(grad_lifted, project, channels)
    padded_shape = (cells_x + 2, cells_y + 2, cells_z + 2, slot_count, 4 * channels)
    returned = with_halo(returning.reshape(padded_shape), (("gx", 0), ("gy", 1), ("gz", 2)), 1)
    grad_hidden = fold_back(returned, 0).reshape(-1, 4 * channels)
    (grad_summed_one,) = back_node_one(
        (grad_hidden[:, :channels] + grad_scalars, grad_hidden[:, channels:])
    )
    grad_own_one, grad_near_one = back_one(grad_summed_one)
    near_grads = (grad_near_one + grad_near_two).T.reshape(
        3, cells_x + 2, cells_y + 2, cells_z + 2, slot_count
    )
    returned_positions = with_halo(near_grads, (("gx", 1), ("gy", 2), ("gz", 3)), 1)
    folded_positions = fold_back(returned_positions, 1).reshape(3, -1)
    forces = -(folded_positions + (grad_own_one + grad_own_two).T).reshape(
        3, cells_x, cells_y, cells_z, slot_count
    )
    return (forces, energy)


def solution(mesh):
    in_specs = (
        P(None, "gx", "gy", "gz", None),
        P("gx", "gy", "gz", None),
        P("gx", "gy", "gz"),
        P(None, "gx", "gy", "gz", None),
        P(),
        P(),
        P(),
        P(),
        P(),
        P(),
        P(),
        P(),
    )
    out_specs = (P(None, "gx", "gy", "gz", None), P())
    return jax.shard_map(body, mesh=mesh, in_specs=in_specs, out_specs=out_specs, check_vma=False)
```

profile of v0, /device:TPU:1, one launch (start us, length us, event | category | flops | bytes accessed | tf_op | source)
XLA Modules:
  0.0 620.7 jit_solution(10241037953944183054)
XLA Ops:
  15.6 4.9 collective-permute-start.2
  20.5 5.8 collective-permute-start.3
  29.8 12.5 %collective-permute-start.5 = (f32[4,4,4,1,16]{4,3,2,1,0:T(1,128)S(1)}, f32[4,4,4,1,16]{4,3,2,1,0:T(1,128)S(1)}, u32[]{:S(2)}, u32[]{:S(2)}) collective-permute-start(f32[4,4,4,1,16]{4,3,2,1,0:T(1,128)S(1)} %get-tuple-element.2903), channel_id=1, source_target_pairs={{1,0},{2,1},{3,2},{4,3},{5,4},{6,5},{7,6},{8,7},{9,8},{10,9},{11,1... | collective-permute-start | bytes 12296 | tf_op jit(solution)/shard_map/ppermute | solution.py:20
  58.3 38.5 %while.143 = (s32[]{:T(128)}, f32[128,512]{1,0:T(8,128)S(1)}, s32[2,512,1]{1,2,0:T(1,128)}, s32[2,512,1]{1,2,0:T(1,128)}, f32[2,512,3]{1,2,0:T(4,128)}, /*index=...) while((s32[]{:T(128)}, f32[128,512]{1,0:T(8,128)S(1)}, ...), condition=%wide.region_3.4_spmd.clone.clone, body=%wide.region_0.3_spmd.clone.clone.sunk | while | flops 23822352 | bytes 16601809 | solution.py:196
  113.8 4.7 collective-permute-done.9
  120.6 9.8 %collective-permute-start.11 = (bf16[4,4,1,16,512]{4,3,2,1,0:T(8,128)(2,1)S(1)}, bf16[4,4,1,16,512]{4,3,2,1,0:T(8,128)(2,1)S(1)}, u32[]{:S(2)}, u32[]{:S(2)}) collective-permute-start(bf16[4,4,1,16,512]{4,3,2,1,0:T(8,128)(2,1)S(1)} %get-tuple-element.2889), channel_id=1, source_target_pairs={{1,0},{2,1},{3,2},{4,3},{5,4},{6,5},{7,6},{8,7},{9,8},{10,9},{11,1... | collective-permute-start | bytes 786440 | tf_op jit(solution)/shard_map/ppermute | solution.py:20
  131.2 9.6 %collective-permute-done.10 = bf16[4,4,1,16,512]{4,3,2,1,0:T(8,128)(2,1)S(1)} collective-permute-done((bf16[4,4,1,16,512]{4,3,2,1,0:T(8,128)(2,1)S(1)}, bf16[4,4,1,16,512]{4,3,2,1,0:T(8,128)(2,1)S(1)}, u32[]{:S(2)}, u32[]{:S(2)}) %collective-permute-start.10) | collective-permute-done | bytes 262176 | tf_op jit(solution)/shard_map/ppermute | solution.py:19
  140.8 11.5 %collective-permute-done.11 = bf16[4,4,1,16,512]{4,3,2,1,0:T(8,128)(2,1)S(1)} collective-permute-done((bf16[4,4,1,16,512]{4,3,2,1,0:T(8,128)(2,1)S(1)}, bf16[4,4,1,16,512]{4,3,2,1,0:T(8,128)(2,1)S(1)}, u32[]{:S(2)}, u32[]{:S(2)}) %collective-permute-start.11) | collective-permute-done | bytes 262176 | tf_op jit(solution)/shard_map/ppermute | solution.py:20
  172.6 58.6 %while.144 = (s32[]{:T(128)}, f32[128,128]{1,0:T(8,128)}, s32[2,512,1]{1,2,0:T(1,128)}, s32[2,512,1]{1,2,0:T(1,128)}, f32[2,512,3]{1,2,0:T(4,128)}, /*index=5*/f...) while((s32[]{:T(128)}, f32[128,128]{1,0:T(8,128)}, ...), condition=%wide.region_7.8_spmd.clone.clone, body=%wide.region_4.7_spmd.clone.clone.sunk | while | flops 22839312 | bytes 9170137 | solution.py:196
  187.5 5.5 scatter_custom_fusion.33
  216.8 5.5 scatter_custom_fusion.33
  235.1 42.0 %while.141 = (s32[]{:T(128)}, f32[1024,3]{1,0:T(8,128)S(1)}, f32[128,3]{1,0:T(8,128)S(1)}, f32[1024,512]{1,0:T(8,128)}, s32[2,512,1]{1,2,0:T(1,128)}, /*index=5*...) while((s32[]{:T(128)}, f32[1024,3]{1,0:T(8,128)S(1)}, ...), condition=%wide.region_16.17_spmd.clone, body=%wide.region_8.16_spmd.clone.sunk | while | flops 24087060 | bytes 15941073 | solution.py:196
  240.3 6.6 %scatter_custom_fusion.28 = f32[1024,512]{1,0:T(8,128)} fusion(f32[1024,512]{1,0:T(8,128)} %get-tuple-element.4021, s32[512]{0:T(512)S(1)} %bitcast.517, f32[512,128]{1,0:T(8,128)S(1)} %get-tuple-element.3636, f32[]{:T(128)} %constant.415.clone.1..sunk, f32[512,128]{1,0:T(8,128)S(1)} %get-tuple-element.3637, ...), kind=kCustom, calls=%fused_computation.28.clone.1 | custom fusion | flops 1048576 | bytes 3146240 | tf_op jit(solution)/shard_map/transpose(jvp())/while/body/eval_jaxpr/scatter-add | solution.py:190
  261.2 6.6 %scatter_custom_fusion.28 = f32[1024,512]{1,0:T(8,128)} fusion(f32[1024,512]{1,0:T(8,128)} %get-tuple-element.4021, s32[512]{0:T(512)S(1)} %bitcast.517, f32[512,128]{1,0:T(8,128)S(1)} %get-tuple-element.3636, f32[]{:T(128)} %constant.415.clone.1..sunk, f32[512,128]{1,0:T(8,128)S(1)} %get-tuple-element.3637, ...), kind=kCustom, calls=%fused_computation.28.clone.1 | custom fusion | flops 1048576 | bytes 3146240 | tf_op jit(solution)/shard_map/transpose(jvp())/while/body/eval_jaxpr/scatter-add | solution.py:190
  296.8 8.6 %collective-permute-done.12 = f32[1,4,4,16,512]{4,3,2,1,0:T(8,128)S(1)} collective-permute-done((f32[1,4,4,16,512]{4,3,2,1,0:T(8,128)}, f32[1,4,4,16,512]{4,3,2,1,0:T(8,128)S(1)}, u32[]{:S(2)}, u32[]{:S(2)}) %collective-permute-start.12) | collective-permute-done | bytes 524320 | tf_op jit(solution)/shard_map/ppermute | solution.py:19
  312.6 8.6 %collective-permute-done.14 = f32[6,1,4,16,512]{4,3,2,1,0:T(8,128)S(1)} collective-permute-done((f32[6,1,4,16,512]{4,3,2,1,0:T(8,128)S(1)}, f32[6,1,4,16,512]{4,3,2,1,0:T(8,128)S(1)}, u32[]{:S(2)}, u32[]{:S(2)}) %collective-permute-start.14) | collective-permute-done | bytes 786464 | tf_op jit(solution)/shard_map/ppermute | solution.py:19
  321.2 10.6 %collective-permute-done.15 = f32[6,1,4,16,512]{4,3,2,1,0:T(8,128)S(1)} collective-permute-done((f32[6,1,4,16,512]{4,3,2,1,0:T(8,128)S(1)}, f32[6,1,4,16,512]{4,3,2,1,0:T(8,128)S(1)}, u32[]{:S(2)}, u32[]{:S(2)}) %collective-permute-start.15) | collective-permute-done | bytes 786464 | tf_op jit(solution)/shard_map/ppermute | solution.py:20
  335.1 9.4 %collective-permute-start.17 = (f32[6,6,1,16,512]{4,3,2,1,0:T(8,128)S(1)}, f32[6,6,1,16,512]{4,3,2,1,0:T(8,128)S(1)}, u32[]{:S(2)}, u32[]{:S(2)}) collective-permute-start(f32[6,6,1,16,512]{4,3,2,1,0:T(8,128)S(1)} %get-tuple-element.2883), channel_id=1, source_target_pairs={{1,0},{2,1},{3,2},{4,3},{5,4},{6,5},{7,6},{8,7},{9,8},{10,9},{11,1... | collective-permute-start | bytes 3538952 | tf_op jit(solution)/shard_map/ppermute | solution.py:20
  344.5 63.2 %collective-permute-done.16 = f32[6,6,1,16,512]{4,3,2,1,0:T(8,128)S(1)} collective-permute-done((f32[6,6,1,16,512]{4,3,2,1,0:T(8,128)S(1)}, f32[6,6,1,16,512]{4,3,2,1,0:T(8,128)S(1)}, u32[]{:S(2)}, u32[]{:S(2)}) %collective-permute-start.16) | collective-permute-done | bytes 1179680 | tf_op jit(solution)/shard_map/ppermute | solution.py:19
  407.7 36.4 %collective-permute-done.17 = f32[6,6,1,16,512]{4,3,2,1,0:T(8,128)S(1)} collective-permute-done((f32[6,6,1,16,512]{4,3,2,1,0:T(8,128)S(1)}, f32[6,6,1,16,512]{4,3,2,1,0:T(8,128)S(1)}, u32[]{:S(2)}, u32[]{:S(2)}) %collective-permute-start.17) | collective-permute-done | bytes 1179680 | tf_op jit(solution)/shard_map/ppermute | solution.py:20
  450.3 34.0 %while.142 = (s32[]{:T(128)}, f32[1024,3]{1,0:T(8,128)S(1)}, f32[128,3]{1,0:T(8,128)S(1)}, s32[2,512,1]{1,2,0:T(1,128)}, f32[2,512,128]{1,2,0:T(8,128)}, /*index...) while((s32[]{:T(128)}, f32[1024,3]{1,0:T(8,128)S(1)}, ...), condition=%wide.region_24.25_spmd.clone, body=%wide.region_17.24_spmd.clone.sunk | while | flops 23431700 | bytes 9132869 | solution.py:196
  486.9 4.6 collective-permute-start.19
  502.0 9.4 %collective-permute-start.23 = (f32[3,6,6,1,16]{4,3,2,1,0:T(1,128)S(1)}, f32[3,6,6,1,16]{4,3,2,1,0:T(1,128)S(1)}, u32[]{:S(2)}, u32[]{:S(2)}) collective-permute-start(f32[3,6,6,1,16]{4,3,2,1,0:T(1,128)S(1)} %get-tuple-element.2893), channel_id=1, source_target_pairs={{1,0},{2,1},{3,2},{4,3},{5,4},{6,5},{7,6},{8,7},{9,8},{10,9},{11,1... | collective-permute-start | bytes 20744 | tf_op jit(solution)/shard_map/ppermute | solution.py:20
  512.2 105.1 %psum.7 = f32[]{:T(128)} all-reduce(f32[]{:T(128)} %fusion.110), channel_id=1, replica_groups=mesh['gx'=4,'gy'=8,'gz'=16] {'gx','gy','gz'}, use_global_device_ids=true, to_apply=%region_26.27 | all-reduce | flops 1 | bytes 8 | tf_op jit(solution)/shard_map/psum | solution.py:225
  (560 shorter events, 276.4 us)
Async XLA Ops:
  2.1 12.8 %collective-permute-start = (f32[4,1,2,2,16]{4,3,2,1,0:T(2,128)S(1)}, f32[4,1,2,2,16]{4,3,2,1,0:T(2,128)S(1)}, u32[]{:S(2)}, u32[]{:S(2)}) collective-permute-start(f32[4,1,2,2,16]{4,3,2,1,0:T(2,128)S(1)} %get-tuple-element.2908), channel_id=1, source_target_pairs={{0,128},{128,256},{256,384},{384,0},{1,129},{129,257},{257,385},{3... | collective-permute-start | bytes 3080 | tf_op jit(solution)/shard_map/ppermute | solution.py:19
  6.0 8.8 %collective-permute-start.1 = (f32[4,1,2,2,16]{4,3,2,1,0:T(2,128)S(1)}, f32[4,1,2,2,16]{4,3,2,1,0:T(2,128)S(1)}, u32[]{:S(2)}, u32[]{:S(2)}) collective-permute-start(f32[4,1,2,2,16]{4,3,2,1,0:T(2,128)S(1)} %get-tuple-element.2909), channel_id=1, source_target_pairs={{128,0},{256,128},{384,256},{0,384},{129,1},{257,129},{385,257},{1... | collective-permute-start | bytes 3080 | tf_op jit(solution)/shard_map/ppermute | solution.py:20
  15.6 11.3 %collective-permute-start.2 = (f32[4,4,1,2,16]{4,3,2,1,0:T(2,128)S(1)}, f32[4,4,1,2,16]{4,3,2,1,0:T(2,128)S(1)}, u32[]{:S(2)}, u32[]{:S(2)}) collective-permute-start(f32[4,4,1,2,16]{4,3,2,1,0:T(2,128)S(1)} %get-tuple-element.2906), channel_id=1, source_target_pairs={{0,16},{16,32},{32,48},{48,64},{64,80},{80,96},{96,112},{112,0},{1... | collective-permute-start | bytes 6152 | tf_op jit(solution)/shard_map/ppermute | solution.py:19
  20.5 6.6 %collective-permute-start.3 = (f32[4,4,1,2,16]{4,3,2,1,0:T(2,128)S(1)}, f32[4,4,1,2,16]{4,3,2,1,0:T(2,128)S(1)}, u32[]{:S(2)}, u32[]{:S(2)}) collective-permute-start(f32[4,4,1,2,16]{4,3,2,1,0:T(2,128)S(1)} %get-tuple-element.2907), channel_id=1, source_target_pairs={{16,0},{32,16},{48,32},{64,48},{80,64},{96,80},{112,96},{0,112},{1... | collective-permute-start | bytes 6152 | tf_op jit(solution)/shard_map/ppermute | solution.py:20
  27.9 18.1 %collective-permute-start.4 = (f32[4,4,4,1,16]{4,3,2,1,0:T(1,128)S(1)}, f32[4,4,4,1,16]{4,3,2,1,0:T(1,128)S(1)}, u32[]{:S(2)}, u32[]{:S(2)}) collective-permute-start(f32[4,4,4,1,16]{4,3,2,1,0:T(1,128)S(1)} %get-tuple-element.2902), channel_id=1, source_target_pairs={{0,1},{1,2},{2,3},{3,4},{4,5},{5,6},{6,7},{7,8},{8,9},{9,10},{10,1... | collective-permute-start | bytes 12296 | tf_op jit(solution)/shard_map/ppermute | solution.py:19
  29.8 16.1 %collective-permute-start.5 = (f32[4,4,4,1,16]{4,3,2,1,0:T(1,128)S(1)}, f32[4,4,4,1,16]{4,3,2,1,0:T(1,128)S(1)}, u32[]{:S(2)}, u32[]{:S(2)}) collective-permute-start(f32[4,4,4,1,16]{4,3,2,1,0:T(1,128)S(1)} %get-tuple-element.2903), channel_id=1, source_target_pairs={{1,0},{2,1},{3,2},{4,3},{5,4},{6,5},{7,6},{8,7},{9,8},{10,9},{11,1... | collective-permute-start | bytes 12296 | tf_op jit(solution)/shard_map/ppermute | solution.py:20
  99.4 6.6 %collective-permute-start.6 = (bf16[1,2,2,16,512]{4,3,2,1,0:T(8,128)(2,1)S(1)}, bf16[1,2,2,16,512]{4,3,2,1,0:T(8,128)(2,1)S(1)}, u32[]{:S(2)}, u32[]{:S(2)}) collective-permute-start(bf16[1,2,2,16,512]{4,3,2,1,0:T(8,128)(2,1)S(1)} %bitcast.544), channel_id=1, source_target_pairs={{0,128},{128,256},{256,384},{384,0},{1,129},{129,257},{257,385},{3... | collective-permute-start | bytes 196616 | tf_op jit(solution)/shard_map/ppermute | solution.py:19
  101.5 5.8 collective-permute-start.7
  107.3 6.5 %collective-permute-start.8 = (bf16[4,1,2,16,512]{4,3,2,1,0:T(8,128)(2,1)S(1)}, bf16[4,1,2,16,512]{4,3,2,1,0:T(8,128)(2,1)S(1)}, u32[]{:S(2)}, u32[]{:S(2)}) collective-permute-start(bf16[4,1,2,16,512]{4,3,2,1,0:T(8,128)(2,1)S(1)} %get-tuple-element.2890), channel_id=1, source_target_pairs={{0,16},{16,32},{32,48},{48,64},{64,80},{80,96},{96,112},{112,0},{1... | collective-permute-start | bytes 393224 | tf_op jit(solution)/shard_map/ppermute | solution.py:19
  110.8 7.7 %collective-permute-start.9 = (bf16[4,1,2,16,512]{4,3,2,1,0:T(8,128)(2,1)S(1)}, bf16[4,1,2,16,512]{4,3,2,1,0:T(8,128)(2,1)S(1)}, u32[]{:S(2)}, u32[]{:S(2)}) collective-permute-start(bf16[4,1,2,16,512]{4,3,2,1,0:T(8,128)(2,1)S(1)} %get-tuple-element.2891), channel_id=1, source_target_pairs={{16,0},{32,16},{48,32},{64,48},{80,64},{96,80},{112,96},{0,112},{1... | collective-permute-start | bytes 393224 | tf_op jit(solution)/shard_map/ppermute | solution.py:20
  118.6 22.2 %collective-permute-start.10 = (bf16[4,4,1,16,512]{4,3,2,1,0:T(8,128)(2,1)S(1)}, bf16[4,4,1,16,512]{4,3,2,1,0:T(8,128)(2,1)S(1)}, u32[]{:S(2)}, u32[]{:S(2)}) collective-permute-start(bf16[4,4,1,16,512]{4,3,2,1,0:T(8,128)(2,1)S(1)} %get-tuple-element.2888), channel_id=1, source_target_pairs={{0,1},{1,2},{2,3},{3,4},{4,5},{5,6},{6,7},{7,8},{8,9},{9,10},{10,1... | collective-permute-start | bytes 786440 | tf_op jit(solution)/shard_map/ppermute | solution.py:19
  120.6 31.8 %collective-permute-start.11 = (bf16[4,4,1,16,512]{4,3,2,1,0:T(8,128)(2,1)S(1)}, bf16[4,4,1,16,512]{4,3,2,1,0:T(8,128)(2,1)S(1)}, u32[]{:S(2)}, u32[]{:S(2)}) collective-permute-start(bf16[4,4,1,16,512]{4,3,2,1,0:T(8,128)(2,1)S(1)} %get-tuple-element.2889), channel_id=1, source_target_pairs={{1,0},{2,1},{3,2},{4,3},{5,4},{6,5},{7,6},{8,7},{9,8},{10,9},{11,1... | collective-permute-start | bytes 786440 | tf_op jit(solution)/shard_map/ppermute | solution.py:20
  287.5 17.8 %collective-permute-start.12 = (f32[1,4,4,16,512]{4,3,2,1,0:T(8,128)}, f32[1,4,4,16,512]{4,3,2,1,0:T(8,128)S(1)}, u32[]{:S(2)}, u32[]{:S(2)}) collective-permute-start(f32[1,4,4,16,512]{4,3,2,1,0:T(8,128)} %bitcast.21), channel_id=1, source_target_pairs={{0,128},{128,256},{256,384},{384,0},{1,129},{129,257},{257,385},{3... | collective-permute-start | bytes 1572872 | tf_op jit(solution)/shard_map/ppermute | solution.py:19
  291.7 15.3 %collective-permute-start.13 = (f32[1,4,4,16,512]{4,3,2,1,0:T(8,128)}, f32[1,4,4,16,512]{4,3,2,1,0:T(8,128)}, u32[]{:S(2)}, u32[]{:S(2)}) collective-permute-start(f32[1,4,4,16,512]{4,3,2,1,0:T(8,128)} %bitcast.23), channel_id=1, source_target_pairs={{128,0},{256,128},{384,256},{0,384},{129,1},{257,129},{385,257},{1... | collective-permute-start | bytes 1572872 | tf_op jit(solution)/shard_map/ppermute | solution.py:20
  308.2 13.0 %collective-permute-start.14 = (f32[6,1,4,16,512]{4,3,2,1,0:T(8,128)S(1)}, f32[6,1,4,16,512]{4,3,2,1,0:T(8,128)S(1)}, u32[]{:S(2)}, u32[]{:S(2)}) collective-permute-start(f32[6,1,4,16,512]{4,3,2,1,0:T(8,128)S(1)} %get-tuple-element.2884), channel_id=1, source_target_pairs={{0,16},{16,32},{32,48},{48,64},{64,80},{80,96},{96,112},{112,0},{1... | collective-permute-start | bytes 2359304 | tf_op jit(solution)/shard_map/ppermute | solution.py:19
  310.1 21.6 %collective-permute-start.15 = (f32[6,1,4,16,512]{4,3,2,1,0:T(8,128)S(1)}, f32[6,1,4,16,512]{4,3,2,1,0:T(8,128)S(1)}, u32[]{:S(2)}, u32[]{:S(2)}) collective-permute-start(f32[6,1,4,16,512]{4,3,2,1,0:T(8,128)S(1)} %get-tuple-element.2885), channel_id=1, source_target_pairs={{16,0},{32,16},{48,32},{64,48},{80,64},{96,80},{112,96},{0,112},{1... | collective-permute-start | bytes 2359304 | tf_op jit(solution)/shard_map/ppermute | solution.py:20
  333.0 74.8 %collective-permute-start.16 = (f32[6,6,1,16,512]{4,3,2,1,0:T(8,128)S(1)}, f32[6,6,1,16,512]{4,3,2,1,0:T(8,128)S(1)}, u32[]{:S(2)}, u32[]{:S(2)}) collective-permute-start(f32[6,6,1,16,512]{4,3,2,1,0:T(8,128)S(1)} %get-tuple-element.2882), channel_id=1, source_target_pairs={{0,1},{1,2},{2,3},{3,4},{4,5},{5,6},{6,7},{7,8},{8,9},{9,10},{10,1... | collective-permute-start | bytes 3538952 | tf_op jit(solution)/shard_map/ppermute | solution.py:19
  335.1 109.1 %collective-permute-start.17 = (f32[6,6,1,16,512]{4,3,2,1,0:T(8,128)S(1)}, f32[6,6,1,16,512]{4,3,2,1,0:T(8,128)S(1)}, u32[]{:S(2)}, u32[]{:S(2)}) collective-permute-start(f32[6,6,1,16,512]{4,3,2,1,0:T(8,128)S(1)} %get-tuple-element.2883), channel_id=1, source_target_pairs={{1,0},{2,1},{3,2},{4,3},{5,4},{6,5},{7,6},{8,7},{9,8},{10,9},{11,1... | collective-permute-start | bytes 3538952 | tf_op jit(solution)/shard_map/ppermute | solution.py:20
  484.9 6.5 %collective-permute-start.18 = (f32[3,1,4,4,16]{4,3,2,1,0:T(4,128)S(1)}, f32[3,1,4,4,16]{4,3,2,1,0:T(4,128)S(1)}, u32[]{:S(2)}, u32[]{:S(2)}) collective-permute-start(f32[3,1,4,4,16]{4,3,2,1,0:T(4,128)S(1)} %get-tuple-element.2898), channel_id=1, source_target_pairs={{0,128},{128,256},{256,384},{384,0},{1,129},{129,257},{257,385},{3... | collective-permute-start | bytes 9224 | tf_op jit(solution)/shard_map/ppermute | solution.py:19
  486.9 5.5 collective-permute-start.19
  492.4 5.1 collective-permute-start.20
  494.3 5.6 collective-permute-start.21
  500.0 118.0 %collective-permute-start.22 = (f32[3,6,6,1,16]{4,3,2,1,0:T(1,128)S(1)}, f32[3,6,6,1,16]{4,3,2,1,0:T(1,128)S(1)}, u32[]{:S(2)}, u32[]{:S(2)}) collective-permute-start(f32[3,6,6,1,16]{4,3,2,1,0:T(1,128)S(1)} %get-tuple-element.2892), channel_id=1, source_target_pairs={{0,1},{1,2},{2,3},{3,4},{4,5},{5,6},{6,7},{7,8},{8,9},{9,10},{10,1... | collective-permute-start | bytes 20744 | tf_op jit(solution)/shard_map/ppermute | solution.py:19
  502.0 116.1 %collective-permute-start.23 = (f32[3,6,6,1,16]{4,3,2,1,0:T(1,128)S(1)}, f32[3,6,6,1,16]{4,3,2,1,0:T(1,128)S(1)}, u32[]{:S(2)}, u32[]{:S(2)}) collective-permute-start(f32[3,6,6,1,16]{4,3,2,1,0:T(1,128)S(1)} %get-tuple-element.2893), channel_id=1, source_target_pairs={{1,0},{2,1},{3,2},{4,3},{5,4},{6,5},{7,6},{8,7},{9,8},{10,9},{11,1... | collective-permute-start | bytes 20744 | tf_op jit(solution)/shard_map/ppermute | solution.py:20
  (100 other events, 800.4 us)
where the time goes:
time: 630 us; the launch traced here: 621 us
  waiting for transfers between devices  160 us (25%)
  other arithmetic  120 us (19%)
  blocking collectives  105 us (17%)
  starting transfers between devices  103 us (16%)
  local copies, waits for them, and re-layouts  97.7 us (16%)
  matrix products  30 us (5%)
    psum x1, blocking collectives, body(): total_energy = lax.psum(local_energy, ('gx', 'gy', 'gz'))  105 us
    ppermute x12, waiting for transfers between devices, with_halo(): before = lax.ppermute(last, axis, up)  90.1 us
    ppermute x12, starting transfers between devices, with_halo(): after = lax.ppermute(initial, axis, down)  71.1 us
    ppermute x12, waiting for transfers between devices, with_halo(): after = lax.ppermute(initial, axis, down)  69.6 us
    ppermute x12, starting transfers between devices, with_halo(): before = lax.ppermute(last, axis, up)  32.2 us
    another operation x46, local copies, waits for them, and re-layouts  29.4 us
    scatter-add x4, other arithmetic, one_block(): jax.ops.segment_sum(message, local_target, own_count)  18.5 us
    dynamic_update_slice x28, local copies, waits for them, and re-layouts, gather_terms(): summed, _ = lax.scan(one_block, initial, pieces)  17.4 us
  transfers between devices with their start and end apart: 24, of which 13 were waited for; matrix products, arithmetic and copies ran while one was open for 2% of the time, Pallas kernels for 0%

commit v1 on v0

v1 whole, which is shorter than its diff:
```python
import functools
import itertools

import jax
import jax.numpy as jnp
from jax import lax
from jax.experimental import pallas as pl
from jax.experimental.pallas import tpu as pltpu
from jax.sharding import PartitionSpec as P

F32 = jnp.float32
BF16 = jnp.bfloat16
MESH = pl.DeviceIdType.MESH
AXES = ("gx", "gy", "gz")

C = 128
CELL = 6.0
DEG = 8
ATOMS = 128
EDGES = 1024
WIDTHS = tuple(0.1 * 30.0 ** (k / 7) for k in range(8))
RSQRT = 1.0 / DEG**0.5

NEIGHBOURS = tuple(d for d in itertools.product((-1, 0, 1), repeat=3) if d != (0, 0, 0))
OWN = {-1: slice(1, 2), 0: slice(1, 3), 1: slice(2, 3)}
THERE = {-1: slice(3, 4), 0: slice(1, 3), 1: slice(0, 1)}
HALO = {-1: slice(0, 1), 0: slice(1, 3), 1: slice(3, 4)}


def dot(a, b, ca, cb):
    return lax.dot_general(a, b, (((ca,), (cb,)), ((), ())), preferred_element_type=F32)


def nn(a, b):
    return dot(a, b, 1, 0)


def tn(a, b):
    return dot(a, b, 0, 0)


def nt(a, b):
    return dot(a, b, 1, 1)


def rows_iota(shape):
    return lax.broadcasted_iota(jnp.int32, shape, 0)


def lanes_iota(shape):
    return lax.broadcasted_iota(jnp.int32, shape, 1)


def mask(condition):
    return jnp.where(condition, 1.0, 0.0).astype(BF16)


def fold(x):
    total = x[:, :ATOMS]
    for r in range(1, DEG):
        total = total + x[:, r * ATOMS : (r + 1) * ATOMS]
    return total


def tile(x):
    return jnp.concatenate([x] * DEG, axis=1)


def sigmoid(x):
    return 1.0 / (1.0 + jnp.exp(-x))


def three(x):
    high = x.astype(BF16)
    rest = x - high.astype(F32)
    middle = rest.astype(BF16)
    return high, middle, (rest - middle.astype(F32)).astype(BF16)


def kernel(
    sizes,
    off,
    spe,
    cnt,
    edg,
    emb,
    rin,
    rhid,
    rout,
    mix1,
    proj,
    mix2,
    rdo,
    frc,
    eng,
    geo,
    geo2,
    srt,
    embp,
    ext,
    gt,
    lg,
    dl,
    rad,
    act,
    usrc,
    g32,
    xs,
    xr,
    ys,
    yr,
    zs,
    zr,
    pg,
    pgx,
    pr,
    esx,
    esy,
    esz,
    geo_s,
    geo_r,
    pos_s,
    pos_r,
    ft_s,
    ft_r,
    gr_s,
    gr_r,
    en_s,
    en_r,
):
    me = tuple(lax.axis_index(a) for a in AXES)

    def at(offset):
        return tuple(lax.rem(m + d + n, n) for m, d, n in zip(me, offset, sizes))

    def remote(src, dst, send, recv, offset):
        return pltpu.make_async_remote_copy(
            src_ref=src,
            dst_ref=dst,
            send_sem=send,
            recv_sem=recv,
            device_id=at(offset),
            device_id_type=MESH,
        )

    def axis_offset(axis, d):
        return tuple(d if k == axis else 0 for k in range(3))

    greeted = list(NEIGHBOURS)
    for axis, n in enumerate(sizes):
        greeted += [axis_offset(axis, d) for d in range(2, n - 1)]
    barrier = pltpu.get_barrier_semaphore()
    for d in greeted:
        pl.semaphore_signal(barrier, inc=1, device_id=at(d), device_id_type=MESH)

    for x, y, z in itertools.product(range(2), repeat=3):
        for k in range(3):
            geo[x + 1, y + 1, z + 1, :, k * 16 : k * 16 + 16] = off[k, x, y, z : z + 1, :]
        geo[x + 1, y + 1, z + 1, :, 48:64] = spe[x, y, z : z + 1, :].astype(F32)
        geo[x + 1, y + 1, z + 1, :, 64:128] = jnp.zeros((1, 64), F32)

    pl.semaphore_wait(barrier, len(greeted))
    pending = []
    geo_copies = []
    for i, (dx, dy, dz) in enumerate(NEIGHBOURS):
        copy = remote(
            geo.at[OWN[dx], OWN[dy], OWN[dz]],
            geo.at[THERE[dx], THERE[dy], THERE[dz]],
            geo_s.at[i],
            geo_r.at[i],
            (dx, dy, dz),
        )
        copy.start()
        geo_copies.append(copy)
    pending += geo_copies

    target = edg[0, 0, 0]
    source = edg[1, 0, 0]
    chosen = mask(rows_iota((ATOMS, EDGES)) == target)
    lane2 = lanes_iota((ATOMS, 2 * ATOMS))
    before = mask((rows_iota((ATOMS, 2 * ATOMS)) < lane2) | (lane2 >= ATOMS))
    high_part = (source >> 3).astype(F32)
    low_part = (source & 7).astype(F32)
    base = jnp.zeros((ATOMS, ATOMS), F32)
    table = jnp.zeros((24, ATOMS), F32)
    for b in range(DEG):
        cut = slice(b * ATOMS, (b + 1) * ATOMS)
        part = chosen[:, cut]
        counted = nn(part, before)
        rank = jnp.sum((counted[:, :ATOMS] + base) * part.astype(F32), axis=0, keepdims=True)
        base = base + counted[:, ATOMS:]
        placed = jnp.where(rows_iota((DEG, ATOMS)).astype(F32) == rank, 1.0, 0.0)
        stacked = jnp.concatenate(
            [placed * high_part[:, cut], placed * low_part[:, cut], placed], axis=0
        ).astype(BF16)
        table = table + nt(stacked, part)
    srt[...] = jnp.where(table[16:24] > 0.5, table[0:8] * 8.0 + table[8:16], -1.0).astype(jnp.int32)
    own_lane = lanes_iota((1, ATOMS))
    own_x, own_y, own_z = (own_lane >> 6, (own_lane >> 5) & 1, (own_lane >> 4) & 1)
    own_index = (((own_x + 1) * 4 + own_y + 1) * 4 + own_z + 1) * 16 + (own_lane & 15)
    srow = jnp.concatenate([srt[r : r + 1, :] for r in range(DEG)] + [own_index], axis=1)
    cell = srow >> 4
    slot = srow & 15
    wide = EDGES + ATOMS
    cells = mask(rows_iota((64, wide)) == cell)
    in_slot = (rows_iota((64, wide)) & 15) == slot

    embp[...] = jnp.zeros((ATOMS, C), F32)
    embp[0:89, :] = emb[...].astype(F32)
    pg[...] = jnp.zeros((64, ATOMS), F32)
    widths = jnp.zeros((8, EDGES), F32)
    for k in range(8):
        widths = jnp.where(rows_iota((8, EDGES)) == k, WIDTHS[k], widths)

    for copy in geo_copies:
        copy.wait_recv()
    for i, (x, y, z) in enumerate(itertools.product(range(4), repeat=3)):
        geo2[i : i + 1, :] = geo[x, y, z]
    table_t = geo2[...].T[:64, :]
    got = jnp.zeros((64, wide), F32)
    for part in three(table_t):
        got = got + nn(part, cells)
    got = jnp.where(in_slot, got, 0.0)
    sums = [jnp.sum(got[k * 16 : k * 16 + 16], axis=0, keepdims=True) for k in range(4)]
    near_cell = cell[:, :EDGES]
    steps = (
        (near_cell >> 4) - 1 - tile(own_x),
        ((near_cell >> 2) & 3) - 1 - tile(own_y),
        (near_cell & 3) - 1 - tile(own_z),
    )
    rel = [
        step.astype(F32) + (s[:, :EDGES] - tile(s[:, EDGES:])) / CELL
        for step, s in zip(steps, sums)
    ]
    squared = rel[0] * rel[0] + rel[1] * rel[1] + rel[2] * rel[2]
    basis = jnp.exp(-squared * widths)
    basis_low = basis.astype(BF16)

    def radial(layer):
        first = tn(rin[layer], basis_low)
        gate = sigmoid(first)
        act[layer, 0] = gate * (1.0 + first * (1.0 - gate))
        second = tn(rhid[layer], (first * gate).astype(BF16))
        gate = sigmoid(second)
        act[layer, 1] = gate * (1.0 + second * (1.0 - gate))
        rad[layer] = tn(rout[layer], (second * gate).astype(BF16))

    def radial_back(layer, grad):
        back = nn(rout[layer], grad).astype(BF16).astype(F32) * act[layer, 1]
        back = nn(rhid[layer], back.astype(BF16)).astype(BF16).astype(F32) * act[layer, 0]
        back = nn(rin[layer], back.astype(BF16)).astype(BF16).astype(F32)
        return -2.0 * jnp.sum(back * widths * basis, axis=0, keepdims=True)

    radial(0)
    kinds = jnp.where(srow[:, :EDGES] >= 0, sums[3][:, :EDGES].astype(jnp.int32), -1)
    usrc[...] = tn(embp[...].astype(BF16), mask(rows_iota((ATOMS, EDGES)) == kinds))
    summed = [fold(rad[0, :C] * usrc[...])]
    vector = rad[0, C:] * usrc[...]
    summed += [fold(vector * rel[k]) for k in range(3)]
    scaled = [(s * RSQRT).astype(BF16) for s in summed]
    mixed = tn(mix1[0], scaled[0])
    mixed_gate = sigmoid(mixed)
    scalars = mixed * mixed_gate
    mixed_slope = mixed_gate * (1.0 + mixed * (1.0 - mixed_gate))
    hidden = [scalars.astype(BF16)] + [tn(mix1[1], s).astype(BF16) for s in scaled[1:]]
    for k in range(4):
        lifted = tn(hidden[k], proj[min(k, 1)]).astype(BF16)
        for i, (x, y, z) in enumerate(itertools.product(range(2), repeat=3)):
            ext[x + 1, y + 1, z + 1, :, k * C : (k + 1) * C] = lifted[i * 16 : i * 16 + 16]

    inner, low, high, every = slice(1, 3), slice(0, 1), slice(3, 4), slice(0, 4)
    numbers = itertools.count()

    def pass_on(axis, direction, others):
        i = next(numbers)
        src, dst = list(others), list(others)
        src.insert(axis, OWN[direction])
        dst.insert(axis, THERE[direction])
        copy = remote(
            ext.at[tuple(src)],
            ext.at[tuple(dst)],
            ft_s.at[i],
            ft_r.at[i],
            axis_offset(axis, direction),
        )
        copy.start()
        pending.append(copy)
        return copy

    both = (-1, 1)
    z_copies = [pass_on(2, d, (inner, inner)) for d in both]
    y_copies = [pass_on(1, d, (inner, inner)) for d in both]
    x_copies = [pass_on(0, d, (inner, inner)) for d in both]
    radial(1)
    for copy, rim in zip(z_copies, (high, low)):
        copy.wait_recv()
        y_copies += [pass_on(1, d, (inner, rim)) for d in both]
        x_copies += [pass_on(0, d, (inner, rim)) for d in both]
    for r in range(DEG):
        cut = slice(r * ATOMS, (r + 1) * ATOMS)
        gt[:, cut] = mask(rows_iota((1024, ATOMS)) == srow[:, cut])
    for copy in y_copies:
        copy.wait_recv()
    for rim in (high, low):
        x_copies += [pass_on(0, d, (rim, every)) for d in both]
    readout = jnp.broadcast_to(rdo[...].reshape(1, C), (C, C)).T
    occupied = jnp.zeros((1, ATOMS), F32)
    for i, (x, y, z) in enumerate(itertools.product(range(2), repeat=3)):
        here = ((own_lane >> 4) == i) & ((own_lane & 15) < cnt[x, y, z])
        occupied = jnp.where(here, 1.0, occupied)
    weight = readout * occupied
    for copy in x_copies:
        copy.wait_recv()

    lg[...] = tn(ext[...].reshape(1024, 4 * C), gt[...])
    inner_sum = rel[0] * lg[C : 2 * C] + rel[1] * lg[2 * C : 3 * C] + rel[2] * lg[3 * C :]
    summed_two = fold(rad[1, :C] * lg[:C] + rad[1, C:] * inner_sum)
    rows = tn(mix2[...], (summed_two * RSQRT).astype(BF16)) + scalars
    gate = sigmoid(rows)
    local = jnp.sum(rows * gate * weight, axis=0, keepdims=True)
    local = jnp.sum(local, axis=1, keepdims=True)
    grad_rows = weight * gate * (1.0 + rows * (1.0 - gate))
    grad = tile(nn(mix2[...], grad_rows.astype(BF16)).astype(BF16).astype(F32) * RSQRT)

    def share(axis, buffer, value, first):
        buffer[me[axis]] = jnp.broadcast_to(value, (1, ATOMS))
        copies = []
        for d in range(1, sizes[axis]):
            here = buffer.at[me[axis]]
            copy = remote(
                here, here, en_s.at[first + d - 1], en_r.at[first + d - 1], axis_offset(axis, d)
            )
            copy.start()
            copies.append(copy)
        pending.extend(copies)
        return copies

    def gathered(axis, buffer, copies):
        for copy in copies:
            copy.wait_recv()
        total = buffer[0]
        for i in range(1, sizes[axis]):
            total = total + buffer[i]
        return total[:, 0:1]

    e_copies = share(0, esx, local, 0)

    grad_inner = grad * rad[1, C:]
    dl[:C] = (grad * rad[1, :C]).astype(BF16)
    for k in range(3):
        dl[(k + 1) * C : (k + 2) * C] = (grad_inner * rel[k]).astype(BF16)

    def grad_copy(i, src, dst, axis, direction):
        copy = remote(src, dst, gr_s.at[i], gr_r.at[i], axis_offset(axis, direction))
        copy.start()
        pending.append(copy)
        return copy

    gx_copies = []
    for i, (slab, d) in enumerate(((0, -1), (3, 1))):
        part = nt(gt[slab * 256 : (slab + 1) * 256, :], dl[...]).astype(BF16)
        xs[i] = part.reshape(4, 4, 16, 4 * C)
        gx_copies.append(grad_copy(i, xs.at[i], xr.at[i], 0, d))
    g32[...] = nt(gt[256:768, :], dl[...]).reshape(2, 4, 4, 16, 4 * C)
    direct = [
        jnp.sum(grad_inner * lg[(k + 1) * C : (k + 2) * C], axis=0, keepdims=True)
        for k in range(3)
    ]
    pull = radial_back(
        1, jnp.concatenate([grad * lg[:C], grad * inner_sum], axis=0).astype(BF16)
    )
    drel = [rel[k] * pull + direct[k] for k in range(3)]

    for i, copy in enumerate(gx_copies):
        copy.wait_recv()
        g32[1 - i] = g32[1 - i] + xr[i].astype(F32)
    gy_copies = []
    for i, (rim, d) in enumerate(((0, -1), (3, 1))):
        ys[i] = g32[:, rim].astype(BF16)
        gy_copies.append(grad_copy(2 + i, ys.at[i], yr.at[i], 1, d))
    e_copies = share(1, esy, gathered(0, esx, e_copies), sizes[0])
    for i, copy in enumerate(gy_copies):
        copy.wait_recv()
        g32[:, 2 - i] = g32[:, 2 - i] + yr[i].astype(F32)
    gz_copies = []
    for i, (rim, d) in enumerate(((0, -1), (3, 1))):
        zs[i] = g32[:, 1:3, rim].astype(BF16)
        gz_copies.append(grad_copy(4 + i, zs.at[i], zr.at[i], 2, d))
    e_copies = share(2, esz, gathered(1, esy, e_copies), sizes[0] + sizes[1])
    for i, copy in enumerate(gz_copies):
        copy.wait_recv()
        g32[:, 1:3, 2 - i] = g32[:, 1:3, 2 - i] + zr[i].astype(F32)

    arrived = g32[:, 1:3, 1:3].reshape(ATOMS, 4 * C)

    def project_back(k):
        block = arrived[:, k * C : (k + 1) * C]
        top = block.astype(BF16)
        rest = (block - top.astype(F32)).astype(BF16)
        weights = proj[min(k, 1)]
        return nt(weights, top) + nt(weights, rest)

    grad_mixed = (project_back(0) + grad_rows) * mixed_slope
    grads = [nn(mix1[0], grad_mixed.astype(BF16))]
    grads += [nn(mix1[1], project_back(k).astype(BF16)) for k in range(1, 4)]
    grads = [tile(g.astype(BF16).astype(F32) * RSQRT) for g in grads]

    towards = rel[0] * grads[1] + rel[1] * grads[2] + rel[2] * grads[3]
    pull = radial_back(
        0, jnp.concatenate([grads[0] * usrc[...], towards * usrc[...]], axis=0).astype(BF16)
    )
    vector = rad[0, C:] * usrc[...]
    drel = [
        drel[k] + rel[k] * pull + jnp.sum(vector * grads[k + 1], axis=0, keepdims=True)
        for k in range(3)
    ]

    moved = []
    for k in range(3):
        here = drel[k] / CELL
        both_ends = jnp.concatenate([here, -fold(here)], axis=1)
        moved.append(jnp.broadcast_to(both_ends, (16, wide)))
    moved.append(jnp.zeros((16, wide), F32))
    spread = jnp.where(in_slot, jnp.concatenate(moved, axis=0), 0.0)
    near = jnp.zeros((64, 64), F32)
    for part in three(spread):
        near = near + nt(cells, part)
    pg[:, 0:64] = near
    for i, (x, y, z) in enumerate(itertools.product(range(4), repeat=3)):
        pgx[x, y, z] = pg[i : i + 1, :]
    pos_copies = []
    for i, (dx, dy, dz) in enumerate(NEIGHBOURS):
        copy = remote(
            pgx.at[HALO[dx], HALO[dy], HALO[dz]],
            pr.at[i, 0 : 2 - abs(dx), 0 : 2 - abs(dy), 0 : 2 - abs(dz)],
            pos_s.at[i],
            pos_r.at[i],
            (dx, dy, dz),
        )
        copy.start()
        pos_copies.append(copy)
    pending += pos_copies
    eng[...] = gathered(2, esz, e_copies) / float(ATOMS * sizes[0] * sizes[1] * sizes[2])
    for copy in pos_copies:
        copy.wait_recv()
    for own in itertools.product(range(2), repeat=3):
        total = pgx[own[0] + 1, own[1] + 1, own[2] + 1]
        for i, d in enumerate(NEIGHBOURS):
            if all(s == 0 or (s == -1) == (o == 1) for s, o in zip(d, own)):
                place = tuple(o if s == 0 else 0 for s, o in zip(d, own))
                total = total + pr[(i,) + place]
        for k in range(3):
            frc[k, own[0], own[1], own[2] : own[2] + 1, :] = -total[:, k * 16 : k * 16 + 16]
    for copy in pending:
        copy.wait_send()


def body(sizes, *args):
    vmem = pl.BlockSpec(memory_space=pltpu.VMEM)
    specs = [vmem] * len(args)
    specs[2] = pl.BlockSpec(memory_space=pltpu.SMEM)
    energy_sends = sum(sizes)
    dma = pltpu.SemaphoreType.DMA
    scratch = [
        pltpu.VMEM((4, 4, 4, 1, 128), F32),
        pltpu.VMEM((64, 128), F32),
        pltpu.VMEM((8, 128), jnp.int32),
        pltpu.VMEM((128, 128), F32),
        pltpu.VMEM((4, 4, 4, 16, 512), BF16),
        pltpu.VMEM((1024, 1024), BF16),
        pltpu.VMEM((512, 1024), F32),
        pltpu.VMEM((512, 1024), BF16),
        pltpu.VMEM((2, 256, 1024), F32),
        pltpu.VMEM((2, 2, 64, 1024), F32),
        pltpu.VMEM((128, 1024), F32),
        pltpu.VMEM((2, 4, 4, 16, 512), F32),
        pltpu.VMEM((2, 4, 4, 16, 512), BF16),
        pltpu.VMEM((2, 4, 4, 16, 512), BF16),
        pltpu.VMEM((2, 2, 4, 16, 512), BF16),
        pltpu.VMEM((2, 2, 4, 16, 512), BF16),
        pltpu.VMEM((2, 2, 2, 16, 512), BF16),
        pltpu.VMEM((2, 2, 2, 16, 512), BF16),
        pltpu.VMEM((64, 128), F32),
        pltpu.VMEM((4, 4, 4, 1, 128), F32),
        pltpu.VMEM((26, 2, 2, 2, 1, 128), F32),
        pltpu.VMEM((sizes[0], 1, 128), F32),
        pltpu.VMEM((sizes[1], 1, 128), F32),
        pltpu.VMEM((sizes[2], 1, 128), F32),
        dma((26,)),
        dma((26,)),
        dma((26,)),
        dma((26,)),
        dma((18,)),
        dma((18,)),
        dma((6,)),
        dma((6,)),
        dma((energy_sends,)),
        dma((energy_sends,)),
    ]
    forces, energy = pl.pallas_call(
        functools.partial(kernel, sizes),
        out_shape=(
            jax.ShapeDtypeStruct(args[0].shape, F32),
            jax.ShapeDtypeStruct((1, 1), F32),
        ),
        in_specs=specs,
        out_specs=(vmem, vmem),
        scratch_shapes=scratch,
        compiler_params=pltpu.CompilerParams(
            collective_id=0, has_side_effects=True, vmem_limit_bytes=48 * 1024 * 1024
        ),
    )(*args)
    return forces, energy.reshape(())


def solution(mesh):
    sizes = tuple(mesh.shape[a] for a in AXES)
    in_specs = (
        P(None, "gx", "gy", "gz", None),
        P("gx", "gy", "gz", None),
        P("gx", "gy", "gz"),
        P(None, "gx", "gy", "gz", None),
    ) + (P(),) * 8
    out_specs = (P(None, "gx", "gy", "gz", None), P())
    return jax.shard_map(
        functools.partial(body, sizes),
        mesh=mesh,
        in_specs=in_specs,
        out_specs=out_specs,
        check_vma=False,
    )
```

time: 630 us -> 94.6 us (0.15); the launches traced: 621 us -> 93.9 us
  waiting for transfers between devices: 160 us -> 0 us
  other arithmetic: 120 us -> 0 us
  blocking collectives: 105 us -> 0 us
  starting transfers between devices: 103 us -> 0 us
  local copies, waits for them, and re-layouts: 97.7 us -> 9.48 us
  Pallas kernels: 0 us -> 82 us
  matrix products: 30 us -> 0 us
    ppermute x24 -> x0, waiting for transfers between devices: 160 us -> none  [the longest x12 90.1 us: with_halo(): before = lax.ppermute(last, axis, up)]
    psum x1 -> x0, blocking collectives: 105 us -> none  [body(): total_energy = lax.psum(local_energy, ('gx', 'gy', 'gz'))]
    ppermute x24 -> x0, starting transfers between devices: 103 us -> none  [the longest x12 71.1 us: with_halo(): after = lax.ppermute(initial, axis, down)]
    pallas_call x0 -> x1, Pallas kernels: none -> 82 us  [body(): pl.pallas_call(functools.partial(kernel, sizes), out_shape=(jax.ShapeDtyp...]
    scatter-add x14 -> x0, other arithmetic: 60.5 us -> none  [the longest x4 18.5 us: one_block(): jax.ops.segment_sum(message, local_target, own_count)]
    dot_general x32 -> x0, matrix products: 30 us -> none  [the longest x8 12.6 us: radial(): jnp.dot(basis_values, w_in, preferred_element_type=jnp.float32)]
    another operation x46 -> x0, local copies, waits for them, and re-layouts: 29.4 us -> none
    gather x18 -> x0, local copies, waits for them, and re-layouts: 20.6 us -> none  [the longest x6 7.04 us: one_block(): features[local_source]]
  transfers between devices with their start and end apart: 24 -> 0, of which waited for: 13 -> 0; matrix products, arithmetic and copies ran while one was open for 2% -> 0% of each run, Pallas kernels for 0% -> 0%
where the time goes in v1:
time: 94.6 us; the launch traced here: 93.9 us
  Pallas kernels  82 us (87%)
  local copies, waits for them, and re-layouts  9.48 us (10%)
  between operations  2.43 us (3%)
    pallas_call x1, Pallas kernels, body(): pl.pallas_call(functools.partial(kernel, sizes), out_shape=(jax.ShapeDtyp...  82 us
    unnamed x25, local copies, waits for them, and re-layouts  9.48 us

profile of v1, /device:TPU:1, one launch (start us, length us, event | category | flops | bytes accessed | tf_op | source)
XLA Modules:
  0.0 93.9 jit_solution(1810822487400557560)
XLA Ops:
  0.6 0.0 copy-start
  0.6 0.8 copy-done
  1.5 0.0 copy-start.1
  1.5 0.8 copy-done.1
  2.3 0.8 copy-done.2
  3.2 0.8 copy-done.3
  3.9 0.0 copy-start.4
  3.9 0.8 copy-done.4
  4.7 0.0 copy-start.5
  4.7 0.7 copy-done.5
  5.4 0.0 copy-start.6
  5.4 0.7 copy-done.6
  6.1 0.0 copy-start.7
  6.1 0.7 copy-done.7
  6.8 0.0 copy-start.8
  6.8 0.7 copy-done.8
  7.5 0.0 copy-start.9
  7.5 0.7 copy-done.9
  8.2 0.0 copy-start.10
  8.2 0.7 copy-done.10
  8.9 0.0 copy-start.11
  8.9 0.7 copy-done.11
  9.5 82.0 %shard_map.131 = (f32[3,2,2,2,16]{4,3,2,1,0:T(2,128)S(1)}, f32[1,1]{1,0:T(1,128)}) custom-call(f32[3,2,2,2,16]{4,3,2,1,0:T(2,128)S(1)} %copy-done.6, s32[2,2,2,16]{3,2,1,0:T(2,128)S(1)} %copy-done.8, s32[2,2,2]{2,1,0:T(2,128)S(1)} %copy-done.10, s32[2,1,1,1,1024]{4,3,2,1,0:T(1,128)S(1)} %copy-done.7, bf16[89,128]{1,0:T(8,128)(2,1)S(1)} %copy-done.5, ...), custom_call_target="tpu_custom_call" | custom-call | tf_op jit(solution)/shard_map/pallas_call | solution.py:500
  91.6 0.6 copy.16
  (2 shorter events, 0.0 us)
Async XLA Ops:
  0.6 0.8 copy-start
  1.5 0.8 copy-start.1
  2.3 0.8 copy-start.2
  3.2 0.8 copy-start.3
  3.9 0.8 copy-start.4
  4.7 0.7 copy-start.5
  5.4 0.7 copy-start.6
  6.1 0.7 copy-start.7
  6.8 0.7 copy-start.8
  7.5 0.7 copy-start.9
  8.2 0.7 copy-start.10
  8.9 0.7 copy-start.11

commit v2 on v1

v2 whole, which is shorter than its diff:
```python
import functools
import itertools

import jax
import jax.numpy as jnp
from jax import lax
from jax.experimental import pallas as pl
from jax.experimental.pallas import tpu as pltpu
from jax.sharding import PartitionSpec as P

F32 = jnp.float32
BF16 = jnp.bfloat16
MESH = pl.DeviceIdType.MESH
AXES = ("gx", "gy", "gz")

C = 128
CELL = 6.0
DEG = 8
ATOMS = 128
EDGES = 1024
WIDTHS = tuple(0.1 * 30.0 ** (k / 7) for k in range(8))
RSQRT = 1.0 / DEG**0.5

NEIGHBOURS = tuple(d for d in itertools.product((-1, 0, 1), repeat=3) if d != (0, 0, 0))
OWN_CELLS = tuple(itertools.product(range(2), repeat=3))
CHUNKS = 8


def place(d):
    return ((d[0] + 1) * 3 + d[1] + 1) * 3 + d[2] + 1


def chunk_of(d):
    return abs(d[0]) * 4 + abs(d[1]) * 2 + abs(d[2])


def dot(a, b, ca, cb):
    return lax.dot_general(a, b, (((ca,), (cb,)), ((), ())), preferred_element_type=F32)


def nn(a, b):
    return dot(a, b, 1, 0)


def tn(a, b):
    return dot(a, b, 0, 0)


def nt(a, b):
    return dot(a, b, 1, 1)


def rows_iota(shape):
    return lax.broadcasted_iota(jnp.int32, shape, 0)


def lanes_iota(shape):
    return lax.broadcasted_iota(jnp.int32, shape, 1)


def mask(condition):
    return jnp.where(condition, 1.0, 0.0).astype(BF16)


def fold(x):
    total = x[:, :ATOMS]
    for r in range(1, DEG):
        total = total + x[:, r * ATOMS : (r + 1) * ATOMS]
    return total


def tile(x):
    return jnp.concatenate([x] * DEG, axis=1)


def silu(x):
    half = 0.5 * x
    up = 1.0 + jnp.tanh(half)
    return half * up, up * (0.5 + half * (1.0 - 0.5 * up))


def two(x):
    high = x.astype(BF16)
    return high, (x - high.astype(F32)).astype(BF16)


def kernel(
    sizes,
    off,
    spe,
    cnt,
    edg,
    emb,
    rin,
    rhid,
    rout,
    mix1,
    proj,
    mix2,
    rdo,
    frc,
    eng,
    vm,
    in_sem,
    blk,
    sel,
    geo,
    srt,
    embp,
    bas,
    rls,
    nqs,
    ohot,
    rad,
    rad2,
    act,
    act2,
    usrc,
    scl,
    gt,
    lg,
    dl,
    gsum,
    drs,
    tgs,
    pgs,
    pgx,
    pr,
    esx,
    esy,
    esz,
    geo_s,
    geo_r,
    pos_s,
    pos_r,
    en_s,
    en_r,
):
    me = tuple(lax.axis_index(a) for a in AXES)
    incoming = (off, spe, cnt, edg, emb, rin, rhid, rout, mix1, proj, mix2, rdo)
    loads = []
    for i, (src, dst) in enumerate(zip(incoming, vm)):
        loads.append(pltpu.make_async_copy(src, dst, in_sem.at[i]))
    for i in (3, 0, 1, 2, 4, 5, 6, 7, 8, 9, 10, 11):
        loads[i].start()
    off, spe, cnt, edg, emb, rin, rhid, rout, mix1, proj, mix2, rdo = vm

    def at(offset):
        return tuple(lax.rem(m + d + n, n) for m, d, n in zip(me, offset, sizes))

    def remote(src, dst, send, recv, offset):
        return pltpu.make_async_remote_copy(
            src_ref=src,
            dst_ref=dst,
            send_sem=send,
            recv_sem=recv,
            device_id=at(offset),
            device_id_type=MESH,
        )

    def axis_offset(axis, d):
        return tuple(d if k == axis else 0 for k in range(3))

    greeted = list(NEIGHBOURS)
    for axis, n in enumerate(sizes):
        greeted += [axis_offset(axis, d) for d in range(2, n - 1)]
    barrier = pltpu.get_barrier_semaphore()
    for d in greeted:
        pl.semaphore_signal(barrier, inc=1, device_id=at(d), device_id_type=MESH)

    loads[3].wait()
    target = edg[0, 0, 0]
    source = edg[1, 0, 0]
    chosen = mask(rows_iota((ATOMS, EDGES)) == target)
    lane2 = lanes_iota((ATOMS, 2 * ATOMS))
    before = mask((rows_iota((ATOMS, 2 * ATOMS)) < lane2) | (lane2 >= ATOMS))
    high_part = (source >> 3).astype(F32)
    low_part = (source & 7).astype(F32)
    base = jnp.zeros((ATOMS, ATOMS), F32)
    table = jnp.zeros((24, ATOMS), F32)
    for b in range(DEG):
        cut = slice(b * ATOMS, (b + 1) * ATOMS)
        part = chosen[:, cut]
        counted = nn(part, before)
        rank = jnp.sum((counted[:, :ATOMS] + base) * part.astype(F32), axis=0, keepdims=True)
        base = base + counted[:, ATOMS:]
        placed = jnp.where(rows_iota((DEG, ATOMS)).astype(F32) == rank, 1.0, 0.0)
        stacked = jnp.concatenate(
            [placed * high_part[:, cut], placed * low_part[:, cut], placed], axis=0
        ).astype(BF16)
        table = table + nt(stacked, part)
    found = table[0:8] * 8.0 + table[8:16] + table[16:24]
    mine = place((0, 0, 0))
    blk[mine, 0:4, :] = found[0:4] * 2048.0 + found[4:8]

    loads[0].wait()
    loads[1].wait()
    for i, (x, y, z) in enumerate(OWN_CELLS):
        here = slice(i * 16, i * 16 + 16)
        for k in range(3):
            blk[mine, 4 + k : 5 + k, here] = off[k, x, y, z : z + 1, :]
        blk[mine, 7:8, here] = spe[x, y, z : z + 1, :].astype(F32)

    pl.semaphore_wait(barrier, len(greeted))
    pending = []
    geo_copies = []
    for i, d in enumerate(NEIGHBOURS):
        there = place(tuple(-k for k in d))
        copy = remote(blk.at[mine], blk.at[there], geo_s.at[i], geo_r.at[i], d)
        copy.start()
        geo_copies.append(copy)
    pending += geo_copies

    for i in (2, 4, 5, 6, 7, 8, 9, 10, 11):
        loads[i].wait()
    embp[...] = jnp.zeros((ATOMS, C), F32)
    embp[0:89, :] = emb[...].astype(F32)
    geo[...] = jnp.zeros((112, ATOMS), F32)
    drs[...] = jnp.zeros((CHUNKS, 8, EDGES), F32)
    widths = jnp.zeros((8, EDGES), F32)
    for k in range(8):
        widths = jnp.where(rows_iota((8, EDGES)) == k, WIDTHS[k], widths)
    own_lane = lanes_iota((1, ATOMS))
    own_cell = (own_lane >> 6, (own_lane >> 5) & 1, (own_lane >> 4) & 1)
    readout = jnp.broadcast_to(rdo[...].reshape(1, C), (C, C)).T
    occupied = jnp.zeros((1, ATOMS), F32)
    for i, (x, y, z) in enumerate(OWN_CELLS):
        here = ((own_lane >> 4) == i) & ((own_lane & 15) < cnt[x, y, z])
        occupied = jnp.where(here, 1.0, occupied)
    weight = readout * occupied

    def lanes_of(d):
        chosen = own_lane >= 0
        for step, cell in zip(d, own_cell):
            if step:
                chosen = chosen & (cell == (0 if step > 0 else 1))
        return chosen

    for copy in geo_copies:
        copy.wait_recv()
    gathered_blocks = [jnp.zeros((8, ATOMS), F32)] * CHUNKS
    for d in itertools.product((-1, 0, 1), repeat=3):
        n = place(d)
        block = blk[n]
        geo[n * 4 : n * 4 + 4, :] = block[4:8]
        a = chunk_of(d)
        gathered_blocks[a] = jnp.where(lanes_of(d), block, gathered_blocks[a])
    for a in range(CHUNKS):
        sel[a] = gathered_blocks[a]
        packed = gathered_blocks[a][0:4].astype(jnp.int32)
        srt[a] = jnp.concatenate([packed >> 11, packed & 2047], axis=0) - 1
    places = two(geo[...])

    def radial(weights, basis_low, act, out):
        first, slope = silu(tn(rin[weights], basis_low))
        act[0] = slope
        second, slope = silu(tn(rhid[weights], first.astype(BF16)))
        act[1] = slope
        out[...] = tn(rout[weights], second.astype(BF16))

    def radial_back(weights, grad, basis, act):
        back = nn(rout[weights], grad) * act[1]
        back = nn(rhid[weights], back.astype(BF16)) * act[0]
        back = nn(rin[weights], back.astype(BF16))
        return -2.0 * jnp.sum(back * widths * basis, axis=0, keepdims=True)

    def forward(a, carry):
        far = ((a >> 2) & 1, (a >> 1) & 1, a & 1)
        srow = jnp.concatenate([srt[a, r : r + 1, :] for r in range(DEG)], axis=1)
        cell = srow >> 4
        near = (cell >> 4, (cell >> 2) & 3, cell & 3)
        cells = [(p + 1) & 1 for p in near]
        atom = ((cells[0] * 2 + cells[1]) * 2 + cells[2]) * 16 + (srow & 15)
        device = jnp.zeros((1, EDGES), jnp.int32)
        for p, f, own in zip(near, far, own_cell):
            device = device * 3 + ((p + 1) >> 1) + tile(f * (1 - 2 * own))
        device = jnp.where(srow >= 0, device, -1)
        nqs[a] = device
        onehot = mask(rows_iota((ATOMS, EDGES)) == atom)
        ohot[a] = onehot
        found = nn(places[0], onehot) + nn(places[1], onehot)
        found = jnp.where((rows_iota((112, EDGES)) >> 2) == device, found, 0.0)
        total = found[0:8]
        for i in range(1, 14):
            total = total + found[i * 8 : i * 8 + 8]
        total = total[0:4] + total[4:8]
        rel = []
        for k in range(3):
            step = (near[k] - 1 - tile(own_cell[k])).astype(F32)
            rel.append(step + (total[k : k + 1] - tile(sel[a, 4 + k : 5 + k, :])) / CELL)
            rls[a, k : k + 1, :] = rel[k]
        squared = rel[0] * rel[0] + rel[1] * rel[1] + rel[2] * rel[2]
        basis = jnp.exp(-squared * widths)
        bas[a] = basis
        radial(0, basis.astype(BF16), act.at[a], rad.at[a])
        kinds = jnp.where(srow >= 0, total[3:4].astype(jnp.int32), -1)
        kept = tn(embp[...].astype(BF16), mask(rows_iota((ATOMS, EDGES)) == kinds))
        usrc[a] = kept
        where = pl.ds(pl.multiple_of(a * ATOMS, ATOMS), ATOMS)
        scl[0:C, where] = (fold(rad[a, :C] * kept) * RSQRT).astype(BF16)
        vector = rad[a, C:] * kept
        for k in range(3):
            scl[(k + 1) * C : (k + 2) * C, where] = (fold(vector * rel[k]) * RSQRT).astype(BF16)
        return carry

    lax.fori_loop(0, CHUNKS, forward, 0)

    scalars, mixed_slope = silu(tn(mix1[0], scl[:C]))
    hidden = [scalars.astype(BF16)]
    hidden += [tn(mix1[1], scl[k * C : (k + 1) * C]).astype(BF16) for k in range(1, 4)]
    lifted = [tn(proj[min(k, 1)], hidden[k]).astype(BF16) for k in range(4)]

    srow = jnp.concatenate([srt[0, r : r + 1, :] for r in range(DEG)], axis=1)
    cell = srow >> 4
    near = (cell >> 4, (cell >> 2) & 3, cell & 3)
    chunk = jnp.zeros((1, EDGES), jnp.int32)
    atom = jnp.zeros((1, EDGES), jnp.int32)
    for p in near:
        chunk = chunk * 2 + 1 - (((p + 1) >> 1) & 1)
        atom = atom * 2 + ((p + 1) & 1)
    row = jnp.where(srow >= 0, chunk * ATOMS + atom * 16 + (srow & 15), -1)
    gt[...] = mask(rows_iota((1024, EDGES)) == row)
    radial(1, bas[0].astype(BF16), act2, rad2)
    rel = [rls[0, k : k + 1, :] for k in range(3)]
    for k in range(4):
        lg[k * C : (k + 1) * C, :] = nn(lifted[k], gt[...])
    inner_sum = rel[0] * lg[C : 2 * C] + rel[1] * lg[2 * C : 3 * C] + rel[2] * lg[3 * C :]
    summed_two = fold(rad2[:C] * lg[:C] + rad2[C:] * inner_sum)
    rows = tn(mix2[...], (summed_two * RSQRT).astype(BF16)) + scalars[:, :ATOMS]
    energy, slope = silu(rows)
    local = jnp.sum(energy * weight, axis=0, keepdims=True)
    local = jnp.sum(local, axis=1, keepdims=True)
    grad_rows = weight * slope
    grad = tile(nn(mix2[...], grad_rows.astype(BF16)) * RSQRT)

    def share(axis, buffer, value, first):
        buffer[me[axis]] = jnp.broadcast_to(value, (1, ATOMS))
        copies = []
        for d in range(1, sizes[axis]):
            here = buffer.at[me[axis]]
            copy = remote(
                here, here, en_s.at[first + d - 1], en_r.at[first + d - 1], axis_offset(axis, d)
            )
            copy.start()
            copies.append(copy)
        pending.extend(copies)
        return copies

    def gathered(axis, buffer, copies):
        for copy in copies:
            copy.wait_recv()
        total = buffer[0]
        for i in range(1, sizes[axis]):
            total = total + buffer[i]
        return total[:, 0:1]

    e_copies = share(0, esx, local, 0)

    grad_inner = grad * rad2[C:]
    dl[:C] = (grad * rad2[:C]).astype(BF16)
    for k in range(3):
        dl[(k + 1) * C : (k + 2) * C] = (grad_inner * rel[k]).astype(BF16)
    back = [nt(dl[k * C : (k + 1) * C], gt[...]) for k in range(4)]
    pull = radial_back(
        1,
        jnp.concatenate([grad * lg[:C], grad * inner_sum], axis=0).astype(BF16),
        bas[0],
        act2,
    )
    for k in range(3):
        direct = jnp.sum(grad_inner * lg[(k + 1) * C : (k + 2) * C], axis=0, keepdims=True)
        drs[0, k : k + 1, :] = rel[k] * pull + direct

    e_copies = share(1, esy, gathered(0, esx, e_copies), sizes[0])
    back = [nn(proj[min(k, 1)], back[k].astype(BF16)) for k in range(4)]
    own_rows = jnp.concatenate([grad_rows, jnp.zeros((C, 1024 - ATOMS), F32)], axis=1)
    back[0] = (back[0] + own_rows) * mixed_slope
    for k in range(4):
        gsum[k * C : (k + 1) * C] = nn(mix1[min(k, 1)], back[k].astype(BF16)) * RSQRT
    pgs[...] = jnp.zeros((112, ATOMS), F32)

    def backward(a, carry):
        where = pl.ds(pl.multiple_of(a * ATOMS, ATOMS), ATOMS)
        grads = [tile(gsum[k * C : (k + 1) * C, where]) for k in range(4)]
        rel = [rls[a, k : k + 1, :] for k in range(3)]
        towards = rel[0] * grads[1] + rel[1] * grads[2] + rel[2] * grads[3]
        kept = usrc[a]
        pull = radial_back(
            0,
            jnp.concatenate([grads[0] * kept, towards * kept], axis=0).astype(BF16),
            bas[a],
            act.at[a],
        )
        vector = rad[a, C:] * kept
        moved = []
        for k in range(3):
            direct = jnp.sum(vector * grads[k + 1], axis=0, keepdims=True)
            moved.append((drs[a, k : k + 1, :] + rel[k] * pull + direct) / CELL)
            tgs[a, k : k + 1, :] = fold(moved[k])
        moved.append(jnp.zeros((1, EDGES), F32))
        moved = jnp.concatenate(moved + moved, axis=0)
        spread = jnp.concatenate([moved] * 14, axis=0)
        spread = jnp.where((rows_iota((112, EDGES)) >> 2) == nqs[a], spread, 0.0)
        onehot = ohot[a]
        top, rest = two(spread)
        pgs[...] += nt(top, onehot) + nt(rest, onehot)
        return carry

    tgs[...] = jnp.zeros((CHUNKS, 4, ATOMS), F32)
    lax.fori_loop(0, 1, backward, 0)
    e_copies = share(2, esz, gathered(1, esy, e_copies), sizes[0] + sizes[1])
    lax.fori_loop(1, CHUNKS, backward, 0)

    pos_copies = []
    for d in itertools.product((-1, 0, 1), repeat=3):
        n = place(d)
        pgx[n] = pgs[n * 4 : n * 4 + 4, :] - jnp.where(lanes_of(d), tgs[chunk_of(d)], 0.0)
    for i, d in enumerate(NEIGHBOURS):
        there = place(tuple(-k for k in d))
        copy = remote(pgx.at[place(d)], pr.at[there], pos_s.at[i], pos_r.at[i], d)
        copy.start()
        pos_copies.append(copy)
    pending += pos_copies
    eng[...] = gathered(2, esz, e_copies) / float(ATOMS * sizes[0] * sizes[1] * sizes[2])
    for copy in pos_copies:
        copy.wait_recv()
    total = pgx[mine]
    for d in NEIGHBOURS:
        total = total + pr[place(d)]
    for i, (x, y, z) in enumerate(OWN_CELLS):
        for k in range(3):
            frc[k, x, y, z : z + 1, :] = -total[k : k + 1, i * 16 : i * 16 + 16]
    for copy in pending:
        copy.wait_send()


def body(sizes, *args):
    hbm = pl.BlockSpec(memory_space=pltpu.HBM)
    vmem = pl.BlockSpec(memory_space=pltpu.VMEM)
    held = [pltpu.VMEM(a.shape, a.dtype) for a in args]
    held[2] = pltpu.SMEM(args[2].shape, args[2].dtype)
    energy_sends = sum(sizes)
    dma = pltpu.SemaphoreType.DMA
    scratch = [
        tuple(held),
        dma((len(args),)),
        pltpu.VMEM((27, 8, 128), F32),
        pltpu.VMEM((8, 8, 128), F32),
        pltpu.VMEM((112, 128), F32),
        pltpu.VMEM((8, 8, 128), jnp.int32),
        pltpu.VMEM((128, 128), F32),
        pltpu.VMEM((8, 8, 1024), F32),
        pltpu.VMEM((8, 3, 1024), F32),
        pltpu.VMEM((8, 1, 1024), jnp.int32),
        pltpu.VMEM((8, 128, 1024), BF16),
        pltpu.VMEM((8, 256, 1024), F32),
        pltpu.VMEM((256, 1024), F32),
        pltpu.VMEM((8, 2, 64, 1024), F32),
        pltpu.VMEM((2, 64, 1024), F32),
        pltpu.VMEM((8, 128, 1024), F32),
        pltpu.VMEM((512, 1024), BF16),
        pltpu.VMEM((1024, 1024), BF16),
        pltpu.VMEM((512, 1024), F32),
        pltpu.VMEM((512, 1024), BF16),
        pltpu.VMEM((512, 1024), F32),
        pltpu.VMEM((8, 8, 1024), F32),
        pltpu.VMEM((8, 4, 128), F32),
        pltpu.VMEM((112, 128), F32),
        pltpu.VMEM((27, 4, 128), F32),
        pltpu.VMEM((27, 4, 128), F32),
        pltpu.VMEM((sizes[0], 1, 128), F32),
        pltpu.VMEM((sizes[1], 1, 128), F32),
        pltpu.VMEM((sizes[2], 1, 128), F32),
        dma((26,)),
        dma((26,)),
        dma((26,)),
        dma((26,)),
        dma((energy_sends,)),
        dma((energy_sends,)),
    ]
    forces, energy = pl.pallas_call(
        functools.partial(kernel, sizes),
        out_shape=(
            jax.ShapeDtypeStruct(args[0].shape, F32),
            jax.ShapeDtypeStruct((1, 1), F32),
        ),
        in_specs=[hbm] * len(args),
        out_specs=(vmem, vmem),
        scratch_shapes=scratch,
        compiler_params=pltpu.CompilerParams(
            collective_id=0, has_side_effects=True, vmem_limit_bytes=62 * 1024 * 1024
        ),
    )(*args)
    return forces, energy.reshape(())


def solution(mesh):
    sizes = tuple(mesh.shape[a] for a in AXES)
    in_specs = (
        P(None, "gx", "gy", "gz", None),
        P("gx", "gy", "gz", None),
        P("gx", "gy", "gz"),
        P(None, "gx", "gy", "gz", None),
    ) + (P(),) * 8
    out_specs = (P(None, "gx", "gy", "gz", None), P())
    return jax.shard_map(
        functools.partial(body, sizes),
        mesh=mesh,
        in_specs=in_specs,
        out_specs=out_specs,
        check_vma=False,
    )
```

time: 94.6 us -> 70 us (0.74)
  Pallas kernels: 82 us -> 66 us
  local copies, waits for them, and re-layouts: 9.48 us -> 1.31 us
    pallas_call x1, Pallas kernels: 82 us -> 66 us  [body(): pl.pallas_call(functools.partial(kernel, sizes), out_shape=(jax.ShapeDtyp...]
    unnamed x25 -> x1, local copies, waits for them, and re-layouts: 9.48 us -> 1.31 us
where the time goes in v2:
time: 70 us; the launch traced here: 69.7 us
  Pallas kernels  66 us (94%)
  between operations  2.41 us (3%)
  local copies, waits for them, and re-layouts  1.31 us (2%)
    pallas_call x1, Pallas kernels, body(): pl.pallas_call(functools.partial(kernel, sizes), out_shape=(jax.ShapeDtyp...  66 us

profile of v2, /device:TPU:1, one launch (start us, length us, event | category | flops | bytes accessed | tf_op | source)
XLA Modules:
  0.0 69.7 jit_solution(9991808682175780431)
XLA Ops:
  0.6 66.0 %shard_map.131 = (f32[3,2,2,2,16]{4,3,2,1,0:T(2,128)}, f32[1,1]{1,0:T(1,128)}) custom-call(f32[3,2,2,2,16]{4,3,2,1,0:T(2,128)} %off.1, s32[2,2,2,16]{3,2,1,0:T(2,128)} %spe.1, s32[2,2,2]{2,1,0:T(2,128)} %cnt.1, s32[2,1,1,1,1024]{4,3,2,1,0:T(1,128)} %edg.1, bf16[89,128]{1,0:T(8,128)(2,1)} %emb.1, bf16[2,8,64]{2,1,0:T(8,128)(2,1)} %rin.1, ...), custom_call_target="tpu_custom_call" | custom-call | tf_op jit(solution)/shard_map/pallas_call | solution.py:481
  66.6 1.3 %copy.16 = f32[3,2,2,2,16]{4,3,2,1,0:T(2,128)} copy(f32[3,2,2,2,16]{4,3,2,1,0:T(2,128)} %get-tuple-element.8) | data formatting | bytes 3072

commit v3 on v2

--- a/solution.py
+++ b/solution.py
@@ -21,9 +21,15 @@
 WIDTHS = tuple(0.1 * 30.0 ** (k / 7) for k in range(8))
 RSQRT = 1.0 / DEG**0.5
 
-NEIGHBOURS = tuple(d for d in itertools.product((-1, 0, 1), repeat=3) if d != (0, 0, 0))
+NEIGHBOURS = tuple(
+    sorted(
+        (d for d in itertools.product((-1, 0, 1), repeat=3) if d != (0, 0, 0)),
+        key=lambda d: (-abs(d[2]), -abs(d[0]) - abs(d[1])),
+    )
+)
 OWN_CELLS = tuple(itertools.product(range(2), repeat=3))
 CHUNKS = 8
+KINDS = 96
 
 
 def place(d):
@@ -73,10 +79,15 @@
     return jnp.concatenate([x] * DEG, axis=1)
 
 
+def silu_of_half(half):
+    up = 1.0 + jnp.tanh(half)
+    value = half * up
+    gate = 0.5 * up
+    return value, gate + value * (1.0 - gate)
+
+
 def silu(x):
-    half = 0.5 * x
-    up = 1.0 + jnp.tanh(half)
-    return half * up, up * (0.5 + half * (1.0 - 0.5 * up))
+    return silu_of_half(0.5 * x)
 
 
 def two(x):
@@ -111,13 +122,14 @@
     rls,
     nqs,
     ohot,
-    rad,
+    vec,
     rad2,
     act,
     act2,
     usrc,
     scl,
     gt,
+    gtt,
     lg,
     dl,
     gsum,
@@ -213,10 +225,11 @@
 
     for i in (2, 4, 5, 6, 7, 8, 9, 10, 11):
         loads[i].wait()
-    embp[...] = jnp.zeros((ATOMS, C), F32)
+    half_in = [(0.5 * rin[k].astype(F32)).astype(BF16) for k in range(2)]
+    half_hid = [(0.5 * rhid[k].astype(F32)).astype(BF16) for k in range(2)]
+    embp[...] = jnp.zeros((KINDS, C), F32)
     embp[0:89, :] = emb[...].astype(F32)
     geo[...] = jnp.zeros((112, ATOMS), F32)
-    drs[...] = jnp.zeros((CHUNKS, 8, EDGES), F32)
     widths = jnp.zeros((8, EDGES), F32)
     for k in range(8):
         widths = jnp.where(rows_iota((8, EDGES)) == k, WIDTHS[k], widths)
@@ -229,6 +242,24 @@
         occupied = jnp.where(here, 1.0, occupied)
     weight = readout * occupied
 
+    source_row = found.astype(jnp.int32) - 1
+    srt[0] = source_row
+    cell = source_row >> 4
+    near = (cell >> 4, (cell >> 2) & 3, cell & 3)
+    chunk = jnp.zeros((DEG, ATOMS), jnp.int32)
+    atom = jnp.zeros((DEG, ATOMS), jnp.int32)
+    for p in near:
+        chunk = chunk * 2 + 1 - (((p + 1) >> 1) & 1)
+        atom = atom * 2 + ((p + 1) & 1)
+    row = jnp.where(source_row >= 0, chunk * ATOMS + atom * 16 + (source_row & 15), -1)
+    srt[1] = row
+    column = row.astype(F32).T
+    for r in range(DEG):
+        cut = slice(r * ATOMS, (r + 1) * ATOMS)
+        gt[:, cut] = mask(rows_iota((1024, ATOMS)) == srt[1, r : r + 1, :])
+        at_lane = lanes_iota((ATOMS, 1024)).astype(F32)
+        gtt[cut, :] = mask(at_lane == column[:, r : r + 1])
+
     def lanes_of(d):
         chosen = own_lane >= 0
         for step, cell in zip(d, own_cell):
@@ -247,16 +278,17 @@
         gathered_blocks[a] = jnp.where(lanes_of(d), block, gathered_blocks[a])
     for a in range(CHUNKS):
         sel[a] = gathered_blocks[a]
-        packed = gathered_blocks[a][0:4].astype(jnp.int32)
-        srt[a] = jnp.concatenate([packed >> 11, packed & 2047], axis=0) - 1
-    places = two(geo[...])
-
-    def radial(weights, basis_low, act, out):
-        first, slope = silu(tn(rin[weights], basis_low))
+        if a:
+            packed = gathered_blocks[a][0:4].astype(jnp.int32)
+            srt[a] = jnp.concatenate([packed >> 11, packed & 2047], axis=0) - 1
+    places = jnp.concatenate(two(geo[...]), axis=1)
+
+    def radial(weights, basis_low, act):
+        first, slope = silu_of_half(tn(half_in[weights], basis_low))
         act[0] = slope
-        second, slope = silu(tn(rhid[weights], first.astype(BF16)))
+        second, slope = silu_of_half(tn(half_hid[weights], first.astype(BF16)))
         act[1] = slope
-        out[...] = tn(rout[weights], second.astype(BF16))
+        return tn(rout[weights], second.astype(BF16))
 
     def radial_back(weights, grad, basis, act):
         back = nn(rout[weights], grad) * act[1]
@@ -264,8 +296,8 @@
         back = nn(rin[weights], back.astype(BF16))
         return -2.0 * jnp.sum(back * widths * basis, axis=0, keepdims=True)
 
-    def forward(a, carry):
-        far = ((a >> 2) & 1, (a >> 1) & 1, a & 1)
+    def forward(a):
+        far = (a >> 2, (a >> 1) & 1, a & 1)
         srow = jnp.concatenate([srt[a, r : r + 1, :] for r in range(DEG)], axis=1)
         cell = srow >> 4
         near = (cell >> 4, (cell >> 2) & 3, cell & 3)
@@ -275,11 +307,12 @@
         for p, f, own in zip(near, far, own_cell):
             device = device * 3 + ((p + 1) >> 1) + tile(f * (1 - 2 * own))
         device = jnp.where(srow >= 0, device, -1)
-        nqs[a] = device
         onehot = mask(rows_iota((ATOMS, EDGES)) == atom)
         ohot[a] = onehot
-        found = nn(places[0], onehot) + nn(places[1], onehot)
-        found = jnp.where((rows_iota((112, EDGES)) >> 2) == device, found, 0.0)
+        found = nn(places, jnp.concatenate([onehot, onehot], axis=0))
+        holds = jnp.where((rows_iota((112, EDGES)) >> 2) == device, 1.0, 0.0)
+        nqs[a] = holds.astype(BF16)
+        found = holds * found
         total = found[0:8]
         for i in range(1, 14):
             total = total + found[i * 8 : i * 8 + 8]
@@ -292,35 +325,26 @@
         squared = rel[0] * rel[0] + rel[1] * rel[1] + rel[2] * rel[2]
         basis = jnp.exp(-squared * widths)
         bas[a] = basis
-        radial(0, basis.astype(BF16), act.at[a], rad.at[a])
+        weights = radial(0, basis.astype(BF16), act.at[a])
         kinds = jnp.where(srow >= 0, total[3:4].astype(jnp.int32), -1)
-        kept = tn(embp[...].astype(BF16), mask(rows_iota((ATOMS, EDGES)) == kinds))
+        kept = tn(embp[...].astype(BF16), mask(rows_iota((KINDS, EDGES)) == kinds))
         usrc[a] = kept
-        where = pl.ds(pl.multiple_of(a * ATOMS, ATOMS), ATOMS)
-        scl[0:C, where] = (fold(rad[a, :C] * kept) * RSQRT).astype(BF16)
-        vector = rad[a, C:] * kept
+        where = slice(a * ATOMS, (a + 1) * ATOMS)
+        scl[0:C, where] = (fold(weights[:C] * kept) * RSQRT).astype(BF16)
+        vector = weights[C:] * kept
+        vec[a] = vector
         for k in range(3):
             scl[(k + 1) * C : (k + 2) * C, where] = (fold(vector * rel[k]) * RSQRT).astype(BF16)
-        return carry
-
-    lax.fori_loop(0, CHUNKS, forward, 0)
+
+    for a in range(CHUNKS):
+        forward(a)
 
     scalars, mixed_slope = silu(tn(mix1[0], scl[:C]))
     hidden = [scalars.astype(BF16)]
     hidden += [tn(mix1[1], scl[k * C : (k + 1) * C]).astype(BF16) for k in range(1, 4)]
     lifted = [tn(proj[min(k, 1)], hidden[k]).astype(BF16) for k in range(4)]
 
-    srow = jnp.concatenate([srt[0, r : r + 1, :] for r in range(DEG)], axis=1)
-    cell = srow >> 4
-    near = (cell >> 4, (cell >> 2) & 3, cell & 3)
-    chunk = jnp.zeros((1, EDGES), jnp.int32)
-    atom = jnp.zeros((1, EDGES), jnp.int32)
-    for p in near:
-        chunk = chunk * 2 + 1 - (((p + 1) >> 1) & 1)
-        atom = atom * 2 + ((p + 1) & 1)
-    row = jnp.where(srow >= 0, chunk * ATOMS + atom * 16 + (srow & 15), -1)
-    gt[...] = mask(rows_iota((1024, EDGES)) == row)
-    radial(1, bas[0].astype(BF16), act2, rad2)
+    rad2[...] = radial(1, bas[0].astype(BF16), act2)
     rel = [rls[0, k : k + 1, :] for k in range(3)]
     for k in range(4):
         lg[k * C : (k + 1) * C, :] = nn(lifted[k], gt[...])
@@ -354,13 +378,13 @@
             total = total + buffer[i]
         return total[:, 0:1]
 
-    e_copies = share(0, esx, local, 0)
+    e_copies = share(2, esz, local, sizes[0] + sizes[1])
 
     grad_inner = grad * rad2[C:]
     dl[:C] = (grad * rad2[:C]).astype(BF16)
     for k in range(3):
         dl[(k + 1) * C : (k + 2) * C] = (grad_inner * rel[k]).astype(BF16)
-    back = [nt(dl[k * C : (k + 1) * C], gt[...]) for k in range(4)]
+    back = [nn(dl[k * C : (k + 1) * C], gtt[...]) for k in range(4)]
     pull = radial_back(
         1,
         jnp.concatenate([grad * lg[:C], grad * inner_sum], axis=0).astype(BF16),
@@ -369,18 +393,16 @@
     )
     for k in range(3):
         direct = jnp.sum(grad_inner * lg[(k + 1) * C : (k + 2) * C], axis=0, keepdims=True)
-        drs[0, k : k + 1, :] = rel[k] * pull + direct
-
-    e_copies = share(1, esy, gathered(0, esx, e_copies), sizes[0])
+        drs[k : k + 1, :] = rel[k] * pull + direct
+
     back = [nn(proj[min(k, 1)], back[k].astype(BF16)) for k in range(4)]
     own_rows = jnp.concatenate([grad_rows, jnp.zeros((C, 1024 - ATOMS), F32)], axis=1)
     back[0] = (back[0] + own_rows) * mixed_slope
     for k in range(4):
         gsum[k * C : (k + 1) * C] = nn(mix1[min(k, 1)], back[k].astype(BF16)) * RSQRT
-    pgs[...] = jnp.zeros((112, ATOMS), F32)
-
-    def backward(a, carry):
-        where = pl.ds(pl.multiple_of(a * ATOMS, ATOMS), ATOMS)
+
+    def backward(a):
+        where = slice(a * ATOMS, (a + 1) * ATOMS)
         grads = [tile(gsum[k * C : (k + 1) * C, where]) for k in range(4)]
         rel = [rls[a, k : k + 1, :] for k in range(3)]
         towards = rel[0] * grads[1] + rel[1] * grads[2] + rel[2] * grads[3]
@@ -391,27 +413,30 @@
             bas[a],
             act.at[a],
         )
-        vector = rad[a, C:] * kept
+        vector = vec[a]
         moved = []
         for k in range(3):
             direct = jnp.sum(vector * grads[k + 1], axis=0, keepdims=True)
-            moved.append((drs[a, k : k + 1, :] + rel[k] * pull + direct) / CELL)
+            pulled = rel[k] * pull + direct
+            if a == 0:
+                pulled = pulled + drs[k : k + 1, :]
+            moved.append(pulled / CELL)
             tgs[a, k : k + 1, :] = fold(moved[k])
         moved.append(jnp.zeros((1, EDGES), F32))
-        moved = jnp.concatenate(moved + moved, axis=0)
-        spread = jnp.concatenate([moved] * 14, axis=0)
-        spread = jnp.where((rows_iota((112, EDGES)) >> 2) == nqs[a], spread, 0.0)
-        onehot = ohot[a]
-        top, rest = two(spread)
-        pgs[...] += nt(top, onehot) + nt(rest, onehot)
-        return carry
+        moved = jnp.concatenate(moved * 4, axis=0).astype(BF16)
+        spread = jnp.concatenate([moved] * 7, axis=0) * nqs[a]
+        return nt(spread, ohot[a])
 
     tgs[...] = jnp.zeros((CHUNKS, 4, ATOMS), F32)
-    lax.fori_loop(0, 1, backward, 0)
-    e_copies = share(2, esz, gathered(1, esy, e_copies), sizes[0] + sizes[1])
-    lax.fori_loop(1, CHUNKS, backward, 0)
+    spreads = []
+    for a in range(CHUNKS):
+        if a == 6:
+            e_copies = share(1, esy, gathered(2, esz, e_copies), sizes[0])
+        spreads.append(backward(a))
+    pgs[...] = sum(spreads)
 
     pos_copies = []
+    e_copies = share(0, esx, gathered(1, esy, e_copies), 0)
     for d in itertools.product((-1, 0, 1), repeat=3):
         n = place(d)
         pgx[n] = pgs[n * 4 : n * 4 + 4, :] - jnp.where(lanes_of(d), tgs[chunk_of(d)], 0.0)
@@ -421,7 +446,6 @@
         copy.start()
         pos_copies.append(copy)
     pending += pos_copies
-    eng[...] = gathered(2, esz, e_copies) / float(ATOMS * sizes[0] * sizes[1] * sizes[2])
     for copy in pos_copies:
         copy.wait_recv()
     total = pgx[mine]
@@ -430,6 +454,7 @@
     for i, (x, y, z) in enumerate(OWN_CELLS):
         for k in range(3):
             frc[k, x, y, z : z + 1, :] = -total[k : k + 1, i * 16 : i * 16 + 16]
+    eng[...] = gathered(0, esx, e_copies) / float(ATOMS * sizes[0] * sizes[1] * sizes[2])
     for copy in pending:
         copy.wait_send()
 
@@ -448,22 +473,23 @@
         pltpu.VMEM((8, 8, 128), F32),
         pltpu.VMEM((112, 128), F32),
         pltpu.VMEM((8, 8, 128), jnp.int32),
-        pltpu.VMEM((128, 128), F32),
+        pltpu.VMEM((96, 128), F32),
         pltpu.VMEM((8, 8, 1024), F32),
         pltpu.VMEM((8, 3, 1024), F32),
-        pltpu.VMEM((8, 1, 1024), jnp.int32),
+        pltpu.VMEM((8, 112, 1024), BF16),
         pltpu.VMEM((8, 128, 1024), BF16),
-        pltpu.VMEM((8, 256, 1024), F32),
+        pltpu.VMEM((8, 128, 1024), F32),
         pltpu.VMEM((256, 1024), F32),
         pltpu.VMEM((8, 2, 64, 1024), F32),
         pltpu.VMEM((2, 64, 1024), F32),
         pltpu.VMEM((8, 128, 1024), F32),
         pltpu.VMEM((512, 1024), BF16),
         pltpu.VMEM((1024, 1024), BF16),
+        pltpu.VMEM((1024, 1024), BF16),
         pltpu.VMEM((512, 1024), F32),
         pltpu.VMEM((512, 1024), BF16),
         pltpu.VMEM((512, 1024), F32),
-        pltpu.VMEM((8, 8, 1024), F32),
+        pltpu.VMEM((8, 1024), F32),
         pltpu.VMEM((8, 4, 128), F32),
         pltpu.VMEM((112, 128), F32),
         pltpu.VMEM((27, 4, 128), F32),

time: 70 us -> 61.8 us (0.88)
  Pallas kernels: 66 us -> 57.8 us
    pallas_call x1, Pallas kernels: 66 us -> 57.8 us  [body(): pl.pallas_call(functools.partial(kernel, sizes), out_shape=(jax.ShapeDtyp...]
where the time goes in v3:
time: 61.8 us; the launch traced here: 61.5 us
  Pallas kernels  57.8 us (94%)
  between operations  2.41 us (4%)
  local copies, waits for them, and re-layouts  1.31 us (2%)
    pallas_call x1, Pallas kernels, body(): pl.pallas_call(functools.partial(kernel, sizes), out_shape=(jax.ShapeDtyp...  57.8 us
    unnamed x1, local copies, waits for them, and re-layouts  1.31 us

profile of v3, /device:TPU:1, one launch (start us, length us, event | category | flops | bytes accessed | tf_op | source)
XLA Modules:
  0.0 61.5 jit_solution(1209867836650441728)
XLA Ops:
  0.6 57.8 %shard_map.131 = (f32[3,2,2,2,16]{4,3,2,1,0:T(2,128)}, f32[1,1]{1,0:T(1,128)}) custom-call(f32[3,2,2,2,16]{4,3,2,1,0:T(2,128)} %off.1, s32[2,2,2,16]{3,2,1,0:T(2,128)} %spe.1, s32[2,2,2]{2,1,0:T(2,128)} %cnt.1, s32[2,1,1,1,1024]{4,3,2,1,0:T(1,128)} %edg.1, bf16[89,128]{1,0:T(8,128)(2,1)} %emb.1, bf16[2,8,64]{2,1,0:T(8,128)(2,1)} %rin.1, ...), custom_call_target="tpu_custom_call" | custom-call | tf_op jit(solution)/shard_map/pallas_call | solution.py:507
  58.5 1.3 %copy.16 = f32[3,2,2,2,16]{4,3,2,1,0:T(2,128)} copy(f32[3,2,2,2,16]{4,3,2,1,0:T(2,128)} %get-tuple-element.8) | data formatting | bytes 3072

commit v4 on v3

--- a/solution.py
+++ b/solution.py
@@ -66,6 +66,10 @@
 
 def mask(condition):
     return jnp.where(condition, 1.0, 0.0).astype(BF16)
+
+
+def hot(rows, wanted):
+    return jnp.where(tile(rows) == wanted.astype(F32).astype(BF16), BF16(1), BF16(0))
 
 
 def fold(x):
@@ -134,6 +138,8 @@
     dl,
     gsum,
     drs,
+    numbered,
+    by_four,
     tgs,
     pgs,
     pgx,
@@ -230,6 +236,9 @@
     embp[...] = jnp.zeros((KINDS, C), F32)
     embp[0:89, :] = emb[...].astype(F32)
     geo[...] = jnp.zeros((112, ATOMS), F32)
+    adds = mask((lanes_iota((8, 3 * C)) >> 7) == rows_iota((8, 3 * C)))
+    numbered[...] = rows_iota((ATOMS, ATOMS)).astype(F32).astype(BF16)
+    by_four[...] = (rows_iota((112, ATOMS)) >> 2).astype(F32).astype(BF16)
     widths = jnp.zeros((8, EDGES), F32)
     for k in range(8):
         widths = jnp.where(rows_iota((8, EDGES)) == k, WIDTHS[k], widths)
@@ -307,12 +316,11 @@
         for p, f, own in zip(near, far, own_cell):
             device = device * 3 + ((p + 1) >> 1) + tile(f * (1 - 2 * own))
         device = jnp.where(srow >= 0, device, -1)
-        onehot = mask(rows_iota((ATOMS, EDGES)) == atom)
+        onehot = hot(numbered[...], atom)
         ohot[a] = onehot
         found = nn(places, jnp.concatenate([onehot, onehot], axis=0))
-        holds = jnp.where((rows_iota((112, EDGES)) >> 2) == device, 1.0, 0.0)
-        nqs[a] = holds.astype(BF16)
-        found = holds * found
+        nqs[a] = hot(by_four[...], device)
+        found = jnp.where((rows_iota((112, EDGES)) >> 2) == device, found, 0.0)
         total = found[0:8]
         for i in range(1, 14):
             total = total + found[i * 8 : i * 8 + 8]
@@ -327,12 +335,12 @@
         bas[a] = basis
         weights = radial(0, basis.astype(BF16), act.at[a])
         kinds = jnp.where(srow >= 0, total[3:4].astype(jnp.int32), -1)
-        kept = tn(embp[...].astype(BF16), mask(rows_iota((KINDS, EDGES)) == kinds))
-        usrc[a] = kept
+        kept = tn(embp[...].astype(BF16), hot(numbered[0:KINDS, :], kinds))
+        usrc[a] = kept.astype(BF16)
         where = slice(a * ATOMS, (a + 1) * ATOMS)
         scl[0:C, where] = (fold(weights[:C] * kept) * RSQRT).astype(BF16)
         vector = weights[C:] * kept
-        vec[a] = vector
+        vec[a] = vector.astype(BF16)
         for k in range(3):
             scl[(k + 1) * C : (k + 2) * C, where] = (fold(vector * rel[k]) * RSQRT).astype(BF16)
 
@@ -346,8 +354,7 @@
 
     rad2[...] = radial(1, bas[0].astype(BF16), act2)
     rel = [rls[0, k : k + 1, :] for k in range(3)]
-    for k in range(4):
-        lg[k * C : (k + 1) * C, :] = nn(lifted[k], gt[...])
+    lg[...] = nn(jnp.concatenate(lifted, axis=0), gt[...])
     inner_sum = rel[0] * lg[C : 2 * C] + rel[1] * lg[2 * C : 3 * C] + rel[2] * lg[3 * C :]
     summed_two = fold(rad2[:C] * lg[:C] + rad2[C:] * inner_sum)
     rows = tn(mix2[...], (summed_two * RSQRT).astype(BF16)) + scalars[:, :ATOMS]
@@ -384,7 +391,7 @@
     dl[:C] = (grad * rad2[:C]).astype(BF16)
     for k in range(3):
         dl[(k + 1) * C : (k + 2) * C] = (grad_inner * rel[k]).astype(BF16)
-    back = [nn(dl[k * C : (k + 1) * C], gtt[...]) for k in range(4)]
+    back = nn(dl[...], gtt[...]).astype(BF16)
     pull = radial_back(
         1,
         jnp.concatenate([grad * lg[:C], grad * inner_sum], axis=0).astype(BF16),
@@ -395,29 +402,31 @@
         direct = jnp.sum(grad_inner * lg[(k + 1) * C : (k + 2) * C], axis=0, keepdims=True)
         drs[k : k + 1, :] = rel[k] * pull + direct
 
-    back = [nn(proj[min(k, 1)], back[k].astype(BF16)) for k in range(4)]
+    back = [nn(proj[min(k, 1)], back[k * C : (k + 1) * C]) for k in range(4)]
     own_rows = jnp.concatenate([grad_rows, jnp.zeros((C, 1024 - ATOMS), F32)], axis=1)
     back[0] = (back[0] + own_rows) * mixed_slope
     for k in range(4):
-        gsum[k * C : (k + 1) * C] = nn(mix1[min(k, 1)], back[k].astype(BF16)) * RSQRT
+        grown = nn(mix1[min(k, 1)], back[k].astype(BF16)) * RSQRT
+        gsum[k * C : (k + 1) * C] = grown.astype(BF16)
 
     def backward(a):
         where = slice(a * ATOMS, (a + 1) * ATOMS)
         grads = [tile(gsum[k * C : (k + 1) * C, where]) for k in range(4)]
         rel = [rls[a, k : k + 1, :] for k in range(3)]
-        towards = rel[0] * grads[1] + rel[1] * grads[2] + rel[2] * grads[3]
+        low = [r.astype(BF16) for r in rel]
+        towards = low[0] * grads[1] + low[1] * grads[2] + low[2] * grads[3]
         kept = usrc[a]
         pull = radial_back(
             0,
-            jnp.concatenate([grads[0] * kept, towards * kept], axis=0).astype(BF16),
+            jnp.concatenate([grads[0] * kept, towards * kept], axis=0),
             bas[a],
             act.at[a],
         )
         vector = vec[a]
+        direct = nn(adds, jnp.concatenate([vector * g for g in grads[1:]], axis=0))
         moved = []
         for k in range(3):
-            direct = jnp.sum(vector * grads[k + 1], axis=0, keepdims=True)
-            pulled = rel[k] * pull + direct
+            pulled = rel[k] * pull + direct[k : k + 1]
             if a == 0:
                 pulled = pulled + drs[k : k + 1, :]
             moved.append(pulled / CELL)
@@ -430,13 +439,10 @@
     tgs[...] = jnp.zeros((CHUNKS, 4, ATOMS), F32)
     spreads = []
     for a in range(CHUNKS):
-        if a == 6:
-            e_copies = share(1, esy, gathered(2, esz, e_copies), sizes[0])
         spreads.append(backward(a))
     pgs[...] = sum(spreads)
 
     pos_copies = []
-    e_copies = share(0, esx, gathered(1, esy, e_copies), 0)
     for d in itertools.product((-1, 0, 1), repeat=3):
         n = place(d)
         pgx[n] = pgs[n * 4 : n * 4 + 4, :] - jnp.where(lanes_of(d), tgs[chunk_of(d)], 0.0)
@@ -446,6 +452,8 @@
         copy.start()
         pos_copies.append(copy)
     pending += pos_copies
+    e_copies = share(1, esy, gathered(2, esz, e_copies), sizes[0])
+    e_copies = share(0, esx, gathered(1, esy, e_copies), 0)
     for copy in pos_copies:
         copy.wait_recv()
     total = pgx[mine]
@@ -478,18 +486,20 @@
         pltpu.VMEM((8, 3, 1024), F32),
         pltpu.VMEM((8, 112, 1024), BF16),
         pltpu.VMEM((8, 128, 1024), BF16),
-        pltpu.VMEM((8, 128, 1024), F32),
+        pltpu.VMEM((8, 128, 1024), BF16),
         pltpu.VMEM((256, 1024), F32),
         pltpu.VMEM((8, 2, 64, 1024), F32),
         pltpu.VMEM((2, 64, 1024), F32),
-        pltpu.VMEM((8, 128, 1024), F32),
+        pltpu.VMEM((8, 128, 1024), BF16),
         pltpu.VMEM((512, 1024), BF16),
         pltpu.VMEM((1024, 1024), BF16),
         pltpu.VMEM((1024, 1024), BF16),
         pltpu.VMEM((512, 1024), F32),
         pltpu.VMEM((512, 1024), BF16),
-        pltpu.VMEM((512, 1024), F32),
+        pltpu.VMEM((512, 1024), BF16),
         pltpu.VMEM((8, 1024), F32),
+        pltpu.VMEM((128, 128), BF16),
+        pltpu.VMEM((112, 128), BF16),
         pltpu.VMEM((8, 4, 128), F32),
         pltpu.VMEM((112, 128), F32),
         pltpu.VMEM((27, 4, 128), F32),

time: 61.8 us -> 56.7 us (0.917)
  Pallas kernels: 57.8 us -> 52.8 us
    pallas_call x1, Pallas kernels: 57.8 us -> 52.8 us  [body(): pl.pallas_call(functools.partial(kernel, sizes), out_shape=(jax.ShapeDtyp...]
where the time goes in v4:
time: 56.7 us; the launch traced here: 56.5 us
  Pallas kernels  52.8 us (93%)
  between operations  2.41 us (4%)
  local copies, waits for them, and re-layouts  1.31 us (2%)
    pallas_call x1, Pallas kernels, body(): pl.pallas_call(functools.partial(kernel, sizes), out_shape=(jax.ShapeDtyp...  52.8 us
    unnamed x1, local copies, waits for them, and re-layouts  1.31 us

profile of v4, /device:TPU:1, one launch (start us, length us, event | category | flops | bytes accessed | tf_op | source)
XLA Modules:
  0.0 56.5 jit_solution(4912610975049236741)
XLA Ops:
  0.6 52.8 %shard_map.131 = (f32[3,2,2,2,16]{4,3,2,1,0:T(2,128)}, f32[1,1]{1,0:T(1,128)}) custom-call(f32[3,2,2,2,16]{4,3,2,1,0:T(2,128)} %off.1, s32[2,2,2,16]{3,2,1,0:T(2,128)} %spe.1, s32[2,2,2]{2,1,0:T(2,128)} %cnt.1, s32[2,1,1,1,1024]{4,3,2,1,0:T(1,128)} %edg.1, bf16[89,128]{1,0:T(8,128)(2,1)} %emb.1, bf16[2,8,64]{2,1,0:T(8,128)(2,1)} %rin.1, ...), custom_call_target="tpu_custom_call" | custom-call | tf_op jit(solution)/shard_map/pallas_call | solution.py:517
  53.4 1.3 %copy.16 = f32[3,2,2,2,16]{4,3,2,1,0:T(2,128)} copy(f32[3,2,2,2,16]{4,3,2,1,0:T(2,128)} %get-tuple-element.8) | data formatting | bytes 3072

commit v5 on v4

--- a/solution.py
+++ b/solution.py
@@ -85,13 +85,35 @@
 
 def silu_of_half(half):
     up = 1.0 + jnp.tanh(half)
+    value = (half * up).astype(BF16)
+    gate = BF16(0.5) * up.astype(BF16)
+    return value, gate + value * (BF16(1) - gate)
+
+
+def silu(x):
+    half = 0.5 * x
+    up = 1.0 + jnp.tanh(half)
     value = half * up
     gate = 0.5 * up
     return value, gate + value * (1.0 - gate)
 
 
-def silu(x):
-    return silu_of_half(0.5 * x)
+def run(steps):
+    while True:
+        try:
+            next(steps)
+        except StopIteration as end:
+            return end.value
+
+
+def in_turns(several, depth):
+    waiting, active = list(several), []
+    while waiting or active:
+        if waiting and len(active) < depth:
+            active.append(waiting.pop(0))
+        for steps in tuple(active):
+            if next(steps, True):
+                active.remove(steps)
 
 
 def two(x):
@@ -233,6 +255,7 @@
         loads[i].wait()
     half_in = [(0.5 * rin[k].astype(F32)).astype(BF16) for k in range(2)]
     half_hid = [(0.5 * rhid[k].astype(F32)).astype(BF16) for k in range(2)]
+    joined = nn(mix1[1], proj[1]).astype(BF16)
     embp[...] = jnp.zeros((KINDS, C), F32)
     embp[0:89, :] = emb[...].astype(F32)
     geo[...] = jnp.zeros((112, ATOMS), F32)
@@ -293,16 +316,25 @@
     places = jnp.concatenate(two(geo[...]), axis=1)
 
     def radial(weights, basis_low, act):
-        first, slope = silu_of_half(tn(half_in[weights], basis_low))
+        first = tn(half_in[weights], basis_low)
+        yield
+        first, slope = silu_of_half(first)
         act[0] = slope
-        second, slope = silu_of_half(tn(half_hid[weights], first.astype(BF16)))
+        second = tn(half_hid[weights], first)
+        yield
+        second, slope = silu_of_half(second)
         act[1] = slope
-        return tn(rout[weights], second.astype(BF16))
+        out = tn(rout[weights], second)
+        yield
+        return out
 
     def radial_back(weights, grad, basis, act):
-        back = nn(rout[weights], grad) * act[1]
-        back = nn(rhid[weights], back.astype(BF16)) * act[0]
-        back = nn(rin[weights], back.astype(BF16))
+        back = nn(rout[weights], grad)
+        yield
+        back = nn(rhid[weights], back.astype(BF16) * act[1])
+        yield
+        back = nn(rin[weights], back.astype(BF16) * act[0])
+        yield
         return -2.0 * jnp.sum(back * widths * basis, axis=0, keepdims=True)
 
     def forward(a):
@@ -319,6 +351,7 @@
         onehot = hot(numbered[...], atom)
         ohot[a] = onehot
         found = nn(places, jnp.concatenate([onehot, onehot], axis=0))
+        yield
         nqs[a] = hot(by_four[...], device)
         found = jnp.where((rows_iota((112, EDGES)) >> 2) == device, found, 0.0)
         total = found[0:8]
@@ -333,7 +366,7 @@
         squared = rel[0] * rel[0] + rel[1] * rel[1] + rel[2] * rel[2]
         basis = jnp.exp(-squared * widths)
         bas[a] = basis
-        weights = radial(0, basis.astype(BF16), act.at[a])
+        weights = yield from radial(0, basis.astype(BF16), act.at[a])
         kinds = jnp.where(srow >= 0, total[3:4].astype(jnp.int32), -1)
         kept = tn(embp[...].astype(BF16), hot(numbered[0:KINDS, :], kinds))
         usrc[a] = kept.astype(BF16)
@@ -344,15 +377,13 @@
         for k in range(3):
             scl[(k + 1) * C : (k + 2) * C, where] = (fold(vector * rel[k]) * RSQRT).astype(BF16)
 
-    for a in range(CHUNKS):
-        forward(a)
+    in_turns([forward(a) for a in range(CHUNKS)], 3)
 
     scalars, mixed_slope = silu(tn(mix1[0], scl[:C]))
-    hidden = [scalars.astype(BF16)]
-    hidden += [tn(mix1[1], scl[k * C : (k + 1) * C]).astype(BF16) for k in range(1, 4)]
-    lifted = [tn(proj[min(k, 1)], hidden[k]).astype(BF16) for k in range(4)]
-
-    rad2[...] = radial(1, bas[0].astype(BF16), act2)
+    lifted = [tn(proj[0], scalars.astype(BF16)).astype(BF16)]
+    lifted += [tn(joined, scl[k * C : (k + 1) * C]).astype(BF16) for k in range(1, 4)]
+
+    rad2[...] = run(radial(1, bas[0].astype(BF16), act2))
     rel = [rls[0, k : k + 1, :] for k in range(3)]
     lg[...] = nn(jnp.concatenate(lifted, axis=0), gt[...])
     inner_sum = rel[0] * lg[C : 2 * C] + rel[1] * lg[2 * C : 3 * C] + rel[2] * lg[3 * C :]
@@ -392,22 +423,24 @@
     for k in range(3):
         dl[(k + 1) * C : (k + 2) * C] = (grad_inner * rel[k]).astype(BF16)
     back = nn(dl[...], gtt[...]).astype(BF16)
-    pull = radial_back(
+    pull = run(
+    radial_back(
         1,
         jnp.concatenate([grad * lg[:C], grad * inner_sum], axis=0).astype(BF16),
         bas[0],
         act2,
     )
+    )
     for k in range(3):
         direct = jnp.sum(grad_inner * lg[(k + 1) * C : (k + 2) * C], axis=0, keepdims=True)
         drs[k : k + 1, :] = rel[k] * pull + direct
 
-    back = [nn(proj[min(k, 1)], back[k * C : (k + 1) * C]) for k in range(4)]
     own_rows = jnp.concatenate([grad_rows, jnp.zeros((C, 1024 - ATOMS), F32)], axis=1)
-    back[0] = (back[0] + own_rows) * mixed_slope
-    for k in range(4):
-        grown = nn(mix1[min(k, 1)], back[k].astype(BF16)) * RSQRT
-        gsum[k * C : (k + 1) * C] = grown.astype(BF16)
+    grad_mixed = (nn(proj[0], back[:C]) + own_rows) * mixed_slope
+    gsum[:C] = (nn(mix1[0], grad_mixed.astype(BF16)) * RSQRT).astype(BF16)
+    for k in range(1, 4):
+        cut = slice(k * C, (k + 1) * C)
+        gsum[cut] = (nn(joined, back[cut]) * RSQRT).astype(BF16)
 
     def backward(a):
         where = slice(a * ATOMS, (a + 1) * ATOMS)
@@ -416,7 +449,7 @@
         low = [r.astype(BF16) for r in rel]
         towards = low[0] * grads[1] + low[1] * grads[2] + low[2] * grads[3]
         kept = usrc[a]
-        pull = radial_back(
+        pull = yield from radial_back(
             0,
             jnp.concatenate([grads[0] * kept, towards * kept], axis=0),
             bas[a],
@@ -434,12 +467,11 @@
         moved.append(jnp.zeros((1, EDGES), F32))
         moved = jnp.concatenate(moved * 4, axis=0).astype(BF16)
         spread = jnp.concatenate([moved] * 7, axis=0) * nqs[a]
-        return nt(spread, ohot[a])
+        spreads.append(nt(spread, ohot[a]))
 
     tgs[...] = jnp.zeros((CHUNKS, 4, ATOMS), F32)
     spreads = []
-    for a in range(CHUNKS):
-        spreads.append(backward(a))
+    in_turns([backward(a) for a in range(CHUNKS)], 3)
     pgs[...] = sum(spreads)
 
     pos_copies = []
@@ -488,8 +520,8 @@
         pltpu.VMEM((8, 128, 1024), BF16),
         pltpu.VMEM((8, 128, 1024), BF16),
         pltpu.VMEM((256, 1024), F32),
-        pltpu.VMEM((8, 2, 64, 1024), F32),
-        pltpu.VMEM((2, 64, 1024), F32),
+        pltpu.VMEM((8, 2, 64, 1024), BF16),
+        pltpu.VMEM((2, 64, 1024), BF16),
         pltpu.VMEM((8, 128, 1024), BF16),
         pltpu.VMEM((512, 1024), BF16),
         pltpu.VMEM((1024, 1024), BF16),

time: 56.7 us -> 55.1 us (0.972)
  Pallas kernels: 52.8 us -> 51.1 us
    pallas_call x1, Pallas kernels: 52.8 us -> 51.1 us  [body(): pl.pallas_call(functools.partial(kernel, sizes), out_shape=(jax.ShapeDtyp...]
where the time goes in v5:
time: 55.1 us; the launch traced here: 54.9 us
  Pallas kernels  51.1 us (93%)
  between operations  2.41 us (4%)
  local copies, waits for them, and re-layouts  1.31 us (2%)
    pallas_call x1, Pallas kernels, body(): pl.pallas_call(functools.partial(kernel, sizes), out_shape=(jax.ShapeDtyp...  51.1 us
    unnamed x1, local copies, waits for them, and re-layouts  1.31 us

profile of v5, /device:TPU:1, one launch (start us, length us, event | category | flops | bytes accessed | tf_op | source)
XLA Modules:
  0.0 54.9 jit_solution(8686784693268084132)
XLA Ops:
  0.6 51.1 %shard_map.131 = (f32[3,2,2,2,16]{4,3,2,1,0:T(2,128)}, f32[1,1]{1,0:T(1,128)}) custom-call(f32[3,2,2,2,16]{4,3,2,1,0:T(2,128)} %off.1, s32[2,2,2,16]{3,2,1,0:T(2,128)} %spe.1, s32[2,2,2]{2,1,0:T(2,128)} %cnt.1, s32[2,1,1,1,1024]{4,3,2,1,0:T(1,128)} %edg.1, bf16[89,128]{1,0:T(8,128)(2,1)} %emb.1, bf16[2,8,64]{2,1,0:T(8,128)(2,1)} %rin.1, ...), custom_call_target="tpu_custom_call" | custom-call | tf_op jit(solution)/shard_map/pallas_call | solution.py:549
  51.8 1.3 %copy.16 = f32[3,2,2,2,16]{4,3,2,1,0:T(2,128)} copy(f32[3,2,2,2,16]{4,3,2,1,0:T(2,128)} %get-tuple-element.8) | data formatting | bytes 3072

commit v6 on v5

--- a/solution.py
+++ b/solution.py
@@ -96,14 +96,6 @@
     value = half * up
     gate = 0.5 * up
     return value, gate + value * (1.0 - gate)
-
-
-def run(steps):
-    while True:
-        try:
-            next(steps)
-        except StopIteration as end:
-            return end.value
 
 
 def in_turns(several, depth):
@@ -377,13 +369,15 @@
         for k in range(3):
             scl[(k + 1) * C : (k + 2) * C, where] = (fold(vector * rel[k]) * RSQRT).astype(BF16)
 
-    in_turns([forward(a) for a in range(CHUNKS)], 3)
+    def weights_two():
+        rad2[...] = yield from radial(1, bas[0].astype(BF16), act2)
+
+    in_turns([forward(a) for a in range(CHUNKS)] + [weights_two()], 3)
 
     scalars, mixed_slope = silu(tn(mix1[0], scl[:C]))
     lifted = [tn(proj[0], scalars.astype(BF16)).astype(BF16)]
     lifted += [tn(joined, scl[k * C : (k + 1) * C]).astype(BF16) for k in range(1, 4)]
 
-    rad2[...] = run(radial(1, bas[0].astype(BF16), act2))
     rel = [rls[0, k : k + 1, :] for k in range(3)]
     lg[...] = nn(jnp.concatenate(lifted, axis=0), gt[...])
     inner_sum = rel[0] * lg[C : 2 * C] + rel[1] * lg[2 * C : 3 * C] + rel[2] * lg[3 * C :]
@@ -423,17 +417,14 @@
     for k in range(3):
         dl[(k + 1) * C : (k + 2) * C] = (grad_inner * rel[k]).astype(BF16)
     back = nn(dl[...], gtt[...]).astype(BF16)
-    pull = run(
-    radial_back(
-        1,
-        jnp.concatenate([grad * lg[:C], grad * inner_sum], axis=0).astype(BF16),
-        bas[0],
-        act2,
-    )
-    )
-    for k in range(3):
-        direct = jnp.sum(grad_inner * lg[(k + 1) * C : (k + 2) * C], axis=0, keepdims=True)
-        drs[k : k + 1, :] = rel[k] * pull + direct
+
+    def backward_two():
+        pull = yield from radial_back(
+            1, jnp.concatenate([grad * lg[:C], grad * inner_sum], axis=0).astype(BF16), bas[0], act2
+        )
+        for k in range(3):
+            direct = jnp.sum(grad_inner * lg[(k + 1) * C : (k + 2) * C], axis=0, keepdims=True)
+            drs[k : k + 1, :] = rel[k] * pull + direct
 
     own_rows = jnp.concatenate([grad_rows, jnp.zeros((C, 1024 - ATOMS), F32)], axis=1)
     grad_mixed = (nn(proj[0], back[:C]) + own_rows) * mixed_slope
@@ -471,7 +462,7 @@
 
     tgs[...] = jnp.zeros((CHUNKS, 4, ATOMS), F32)
     spreads = []
-    in_turns([backward(a) for a in range(CHUNKS)], 3)
+    in_turns([backward_two()] + [backward(a) for a in (1, 2, 3, 4, 5, 6, 7, 0)], 3)
     pgs[...] = sum(spreads)
 
     pos_copies = []
@@ -480,7 +471,9 @@
         pgx[n] = pgs[n * 4 : n * 4 + 4, :] - jnp.where(lanes_of(d), tgs[chunk_of(d)], 0.0)
     for i, d in enumerate(NEIGHBOURS):
         there = place(tuple(-k for k in d))
-        copy = remote(pgx.at[place(d)], pr.at[there], pos_s.at[i], pos_r.at[i], d)
+        copy = remote(
+            pgx.at[place(d), 0:3], pr.at[there, 0:3], pos_s.at[i], pos_r.at[i], d
+        )
         copy.start()
         pos_copies.append(copy)
     pending += pos_copies
@@ -488,9 +481,9 @@
     e_copies = share(0, esx, gathered(1, esy, e_copies), 0)
     for copy in pos_copies:
         copy.wait_recv()
-    total = pgx[mine]
+    total = pgx[mine, 0:3, :]
     for d in NEIGHBOURS:
-        total = total + pr[place(d)]
+        total = total + pr[place(d), 0:3, :]
     for i, (x, y, z) in enumerate(OWN_CELLS):
         for k in range(3):
             frc[k, x, y, z : z + 1, :] = -total[k : k + 1, i * 16 : i * 16 + 16]

time: 55.1 us -> 54.6 us (level)
  no operation moved by 1% of the time
where the time goes in v6:
time: 54.6 us; the launch traced here: 54.3 us
  Pallas kernels  50.6 us (93%)
  between operations  2.41 us (4%)
  local copies, waits for them, and re-layouts  1.31 us (2%)
    pallas_call x1, Pallas kernels, body(): pl.pallas_call(functools.partial(kernel, sizes), out_shape=(jax.ShapeDtyp...  50.6 us
    unnamed x1, local copies, waits for them, and re-layouts  1.31 us

profile of v6, /device:TPU:1, one launch (start us, length us, event | category | flops | bytes accessed | tf_op | source)
XLA Modules:
  0.0 54.3 jit_solution(8094265273786786662)
XLA Ops:
  0.6 50.6 %shard_map.131 = (f32[3,2,2,2,16]{4,3,2,1,0:T(2,128)}, f32[1,1]{1,0:T(1,128)}) custom-call(f32[3,2,2,2,16]{4,3,2,1,0:T(2,128)} %off.1, s32[2,2,2,16]{3,2,1,0:T(2,128)} %spe.1, s32[2,2,2]{2,1,0:T(2,128)} %cnt.1, s32[2,1,1,1,1024]{4,3,2,1,0:T(1,128)} %edg.1, bf16[89,128]{1,0:T(8,128)(2,1)} %emb.1, bf16[2,8,64]{2,1,0:T(8,128)(2,1)} %rin.1, ...), custom_call_target="tpu_custom_call" | custom-call | tf_op jit(solution)/shard_map/pallas_call | solution.py:542
  51.3 1.3 %copy.16 = f32[3,2,2,2,16]{4,3,2,1,0:T(2,128)} copy(f32[3,2,2,2,16]{4,3,2,1,0:T(2,128)} %get-tuple-element.8) | data formatting | bytes 3072

commit v7 on v6

--- a/solution.py
+++ b/solution.py
@@ -422,9 +422,10 @@
         pull = yield from radial_back(
             1, jnp.concatenate([grad * lg[:C], grad * inner_sum], axis=0).astype(BF16), bas[0], act2
         )
+        parts = [(grad_inner * lg[(k + 1) * C : (k + 2) * C]).astype(BF16) for k in range(3)]
+        direct = nn(adds, jnp.concatenate(parts, axis=0))
         for k in range(3):
-            direct = jnp.sum(grad_inner * lg[(k + 1) * C : (k + 2) * C], axis=0, keepdims=True)
-            drs[k : k + 1, :] = rel[k] * pull + direct
+            drs[k : k + 1, :] = rel[k] * pull + direct[k : k + 1]
 
     own_rows = jnp.concatenate([grad_rows, jnp.zeros((C, 1024 - ATOMS), F32)], axis=1)
     grad_mixed = (nn(proj[0], back[:C]) + own_rows) * mixed_slope

time: 54.6 us -> 54.5 us (level)
  no operation moved by 1% of the time
where the time goes in v7:
time: 54.5 us; the launch traced here: 54.2 us
  Pallas kernels  50.5 us (93%)
  between operations  2.41 us (4%)
  local copies, waits for them, and re-layouts  1.31 us (2%)
    pallas_call x1, Pallas kernels, body(): pl.pallas_call(functools.partial(kernel, sizes), out_shape=(jax.ShapeDtyp...  50.5 us
    unnamed x1, local copies, waits for them, and re-layouts  1.31 us

profile of v7, /device:TPU:1, one launch (start us, length us, event | category | flops | bytes accessed | tf_op | source)
XLA Modules:
  0.0 54.2 jit_solution(18162136779561552824)
XLA Ops:
  0.6 50.5 %shard_map.131 = (f32[3,2,2,2,16]{4,3,2,1,0:T(2,128)}, f32[1,1]{1,0:T(1,128)}) custom-call(f32[3,2,2,2,16]{4,3,2,1,0:T(2,128)} %off.1, s32[2,2,2,16]{3,2,1,0:T(2,128)} %spe.1, s32[2,2,2]{2,1,0:T(2,128)} %cnt.1, s32[2,1,1,1,1024]{4,3,2,1,0:T(1,128)} %edg.1, bf16[89,128]{1,0:T(8,128)(2,1)} %emb.1, bf16[2,8,64]{2,1,0:T(8,128)(2,1)} %rin.1, ...), custom_call_target="tpu_custom_call" | custom-call | tf_op jit(solution)/shard_map/pallas_call | solution.py:543
  51.1 1.3 %copy.16 = f32[3,2,2,2,16]{4,3,2,1,0:T(2,128)} copy(f32[3,2,2,2,16]{4,3,2,1,0:T(2,128)} %get-tuple-element.8) | data formatting | bytes 3072
